TPU v7x, 32 devices: a whole 2x2x4 slice. The times are simulated.
32 devices in a mesh: dp: 8 (over z, y), ctx: 4 (over x, core).
Axes of the slice: x: 2, y: 2, z: 4, core: 2. Of those that a mesh axis runs over, the one named last changes fastest.
Arguments:
- tokens: bfloat16 [2, 4096, 1088], P(None, ('dp', 'ctx')), may hold values from -6 to 6
- cotangent: bfloat16 [2, 4096, 1088], P(None, ('dp', 'ctx')), may hold values from -6 to 6
- w_attn: bfloat16 [1088, 4352], P(None, ('dp', 'ctx'))
- w_up: bfloat16 [1088, 4352], P(None, ('dp', 'ctx')), may hold values from -0.1875 to 0.1875
- w_down: bfloat16 [4352, 1088], P(('dp', 'ctx')), may hold values from -0.09375 to 0.09375
- vectors: bfloat16 [13056], P(('dp', 'ctx'))
- segments: int32 [2, 8, 512], P(None, 'dp'), may hold values from 0 to 511, as said below
Outputs:
- mixed: bfloat16 [2, 4096, 1088], P(None, ('dp', 'ctx'))
- input_grad: bfloat16 [2, 4096, 1088], P(None, ('dp', 'ctx'))
- attn_grad: float32 [1088, 4352], P(None, ('dp', 'ctx'))
- up_grad: float32 [1088, 4352], P(None, ('dp', 'ctx'))
- down_grad: float32 [4352, 1088], P(('dp', 'ctx'))
- vector_grad: float32 [13056], P(('dp', 'ctx'))
Inputs may be any that keep to these rules, and one draw needn't show every extreme that they name: `segments`: entries never fall along a group's rows; each equals the row where its sequence starts (the first row of a group starts one; a sequence may be a single row). In every group and micro-batch one sequence has rows on the first and the last of the group's ctx devices.
All inputs are finite; a program needn't handle non-finite values.
Results may differ from a plain program's by a relative error of at most 0.014.
Values may be sent and summed in bfloat16 or wider, within the bound.
No kernel may reach another device: no remote copies, remote signals or barrier semaphores. Data moves between devices by JAX's collectives and lax.ppermute only.
A program may use at most 256 MiB of HBM per device.

v0:
```python
from functools import partial

import jax
import jax.numpy as jnp
from jax import lax
from jax.experimental import pallas as pl
from jax.experimental.layout import Layout, with_layout_constraint
from jax.experimental.pallas import tpu as pltpu
from jax.sharding import PartitionSpec as P

HEAD_DIM = 64
HALO = 32
BODY = 128
NEG_FILL = -1e30
EPSILON = 1e-05
BF = jnp.bfloat16
F32 = jnp.float32
BOTH = ("dp", "ctx")
CORE_PAIRS = [(0, 1), (1, 0), (2, 3), (3, 2)]
CHIP_PAIRS = [(0, 2), (2, 0), (1, 3), (3, 1)]
BLOCKS = (0, 2, 1, 3)
SHIFTS = (0, 1, 3, 2)
ORDER = ((2, 1), (2, 0), (0, 0), (0, 1), (1, 0), (1, 1), (3, 0), (3, 1))
THIRDS = (64, 160)
CUT = 144
BACK_CUT = 112
SIDE_PAIRS = [(p, p ^ 1) for p in range(8)]


def shift_pairs(step):
    return [(z * 2 + y, ((z + step) % 4) * 2 + y) for z in range(4) for y in range(2)]


def dot(left, right, left_dim, right_dim):
    return lax.dot_general(
        left, right, (((left_dim,), (right_dim,)), ((), ())), preferred_element_type=F32
    )


def norm_stats(values):
    centred = values - jnp.mean(values, axis=-1, keepdims=True)
    scale = lax.rsqrt(jnp.mean(centred * centred, axis=-1, keepdims=True) + EPSILON)
    return centred * scale, scale


def norm_pull(grad, hat, scale, gain):
    grad_hat = grad * gain
    along = jnp.mean(grad_hat * hat, axis=-1, keepdims=True)
    return scale * (grad_hat - jnp.mean(grad_hat, axis=-1, keepdims=True) - hat * along)


def row_major(value):
    return with_layout_constraint(value, Layout(tuple(range(value.ndim))))


def send(value, axes, pairs):
    rows = value.shape[-2]
    if rows % 16:
        return lax.ppermute(value, axes, pairs)
    cut = value.reshape(value.shape[:-2] + (rows // 16, 16, value.shape[-1]))
    return lax.ppermute(cut, axes, pairs).reshape(value.shape)


def hold(values, *others):
    return lax.optimization_barrier(tuple(values) + tuple(others))[: len(values)]


def to_core(value):
    return send(value, "ctx", CORE_PAIRS)


def to_chip(value):
    return send(value, "ctx", CHIP_PAIRS)


def to_side(value):
    return send(value, "dp", SIDE_PAIRS)


def to_shift(value, step, back=False):
    pairs = shift_pairs(step)
    return send(value, "dp", [(b, a) for a, b in pairs] if back else pairs)


def row_gather(mine):
    across = to_chip(mine)
    return [mine, across, to_core(mine), to_core(across)]


def half_sum(other, arrived):
    rows = other.shape[1]
    return (other.astype(F32) + arrived[:, rows:].astype(F32)).astype(BF)


def row_scatter(keep, other, away):
    arrived = to_core(away)
    return keep, arrived, to_chip(half_sum(other, arrived))


def dp_order(z, y):
    return [((z - k) % 4) * 2 + (y ^ s) for k, s in ORDER]


def pick(stacked, index):
    return lax.dynamic_index_in_dim(stacked, index, axis=0, keepdims=False)


def reorder(table, order):
    hot = (order[:, None] == jnp.arange(table.shape[0])[None, :]).astype(F32)
    return jnp.sum(hot[:, :, None] * table[None], axis=1)


def reorder_back(table, order):
    hot = (order[:, None] == jnp.arange(table.shape[0])[None, :]).astype(F32)
    return jnp.sum(hot[:, :, None] * table[:, None, :], axis=0)


def ctx_table(mine, ctx):
    across = lax.ppermute(mine[None], "ctx", CHIP_PAIRS)
    pair = jnp.concatenate([mine[None], across], axis=0)
    table = jnp.concatenate([pair, lax.ppermute(pair, "ctx", CORE_PAIRS)], axis=0)
    return reorder_back(table.astype(F32), jnp.stack([ctx ^ j for j in BLOCKS]))


def head_rows(table, ctx, last):
    middle = 8 * HEAD_DIM
    first = lax.dynamic_slice_in_dim(table, 128 * ctx, 128, axis=0)
    second = lax.dynamic_slice_in_dim(table, middle + HEAD_DIM + 128 * ctx, 128, axis=0)
    mid = table[middle : middle + HEAD_DIM]
    return jnp.concatenate([first, second, jnp.where(last, mid, jnp.zeros_like(mid))], axis=0)


def head_rows_back(mine, ctx, last):
    middle = 8 * HEAD_DIM
    table = jnp.zeros((2 * middle + HEAD_DIM,) + mine.shape[1:], mine.dtype)
    table = lax.dynamic_update_slice_in_dim(table, mine[:128], 128 * ctx, axis=0)
    table = lax.dynamic_update_slice_in_dim(
        table, mine[128:256], middle + HEAD_DIM + 128 * ctx, axis=0
    )
    mid = jnp.where(last, mine[256:], jnp.zeros_like(mine[256:]))
    return lax.dynamic_update_slice_in_dim(table, mid, middle, axis=0)


def gelu_parts(hidden):
    factor = 0.7978845608028654
    square = hidden * hidden
    bent = jnp.tanh(factor * hidden * (1.0 + 0.044715 * square))
    active = 0.5 * hidden * (1.0 + bent)
    slope = 0.5 * (1.0 + bent) + 0.5 * hidden * (1.0 - bent * bent) * factor * (
        1.0 + 3 * 0.044715 * square
    )
    return active, slope


def full(shape):
    return pl.BlockSpec(shape, lambda *_: (0,) * len(shape))


def per(shape, step=1):
    return pl.BlockSpec((1,) + shape, lambda i: (i // step,) + (0,) * len(shape))


def params(mib):
    return pltpu.CompilerParams(vmem_limit_bytes=mib * 1024 * 1024)


def whole(array):
    return full(array.shape)


SCALARS = pl.BlockSpec(memory_space=pltpu.SMEM)


def shape_of(dtype, *dims):
    return jax.ShapeDtypeStruct(dims, dtype)


def head_places(shape, axis, ctx):
    own = lax.broadcasted_iota(jnp.int32, shape, axis)
    middle = 8 * HEAD_DIM
    shift = jnp.where(own < BODY, BODY * ctx, middle + HEAD_DIM - BODY + BODY * ctx)
    shift = jnp.where(own < 2 * BODY, shift, middle - 2 * BODY)
    return jnp.where((own < 2 * BODY) | (ctx == 3), own + shift, -1)


def write_halves(values, rows, keep_ref, other_ref, send_ref):
    keep_ref[0] = values[:rows]
    other_ref[0] = values[rows : 2 * rows].astype(BF)
    send_ref[0] = values[2 * rows :].astype(BF)


def assemble(place_ref, near, side, weight_ref):
    width = weight_ref.shape[0] // 4
    z, y = place_ref[0], place_ref[1]
    for k, pair in zip(SHIFTS, zip(near, side)):
        region = lax.rem(z + 4 - k, 4) * width
        for block_ref, half in zip(pair, (y, 1 - y)):
            to = pl.multiple_of(region + BODY * half, HEAD_DIM)
            weight_ref[pl.ds(to, BODY), :] = block_ref[:BODY, :]
            to = pl.multiple_of(region + 2 * BODY + HALO * half, HALO)
            weight_ref[pl.ds(to, HALO), :] = block_ref[BODY : BODY + HALO, :]


def write_mask(row_ref, mask_ref):
    row = row_ref[0].astype(F32)
    first, own = row[0:1], row[1:2]
    square = (128, row.shape[1])
    first_col = jnp.transpose(jnp.broadcast_to(first, square))[:, :1]
    own_col = jnp.transpose(jnp.broadcast_to(own, square))[:, :1]
    allowed = (own <= own_col) & (first == first_col)
    mask_ref[...] = jnp.where(allowed, 0.0, NEG_FILL)


def attend_kernel(
    place_ref, x0, x1, x2, x3, n0, n1, n2, n3, s0, s1, s2, s3, row_ref,
    normed_ref, qkv_ref, log_ref, heads_ref, vec_ref, line_ref,
    keep_ref, other_ref, send_ref, weight_ref, mask_ref, bias_ref,
):
    width = heads_ref.shape[2]
    count = width // HEAD_DIM
    model = vec_ref.shape[1]
    part = model // 2
    rows = x0.shape[1]

    @pl.when(pl.program_id(0) == 0)
    def _():
        z, y, ctx = place_ref[0], place_ref[1], place_ref[2]
        assemble(place_ref, (n0, n1, n2, n3), (s0, s1, s2, s3), weight_ref)
        for k, pair in zip(SHIFTS, ((n0, s0), (n1, s1), (n2, s2), (n3, s3))):
            owner = lax.rem(z + 4 - k, 4)
            for block_ref, half in zip(pair, (y, 1 - y)):
                lines = block_ref[BODY + HALO :, :].astype(F32)
                for i in range(3):
                    line_ref[pl.ds(3 * (2 * owner + half) + i, 1), :] = lines[i : i + 1, :part]
        for i in range(8):
            vec_ref[i : i + 1, :part] = line_ref[2 * i : 2 * i + 1, :]
            vec_ref[i : i + 1, part:] = line_ref[2 * i + 1 : 2 * i + 2, :]
        own = head_places((model, width), 1, ctx)
        hot = (lax.broadcasted_iota(jnp.int32, (model, width), 0) == own).astype(F32).astype(BF)
        own_vec = dot(vec_ref[...].astype(BF), hot, 1, 0)
        bias_ref[:, :width] = own_vec[2:3]
        bias_ref[:, width : 2 * width] = jnp.zeros((1, width), F32)
        bias_ref[:, 2 * width :] = own_vec[3:4]

    gain, bias = vec_ref[0:1, :], vec_ref[1:2, :]
    for i, x_ref in enumerate((x0, x1, x2, x3)):
        hat, _ = norm_stats(x_ref[0].astype(F32))
        normed_ref[0, i * rows : (i + 1) * rows, :] = (hat * gain + bias).astype(BF)
    normed = normed_ref[0]
    qkv_ref[0] = (dot(normed, weight_ref[: 3 * width, :], 1, 1) + bias_ref[...]).astype(BF)
    write_mask(row_ref, mask_ref)
    for head in range(count):
        lanes = [slice(i * width + head * HEAD_DIM, i * width + (head + 1) * HEAD_DIM) for i in range(3)]
        queries, keys, values = [qkv_ref[0, :, part] for part in lanes]
        queries = queries * jnp.asarray(HEAD_DIM ** (-0.5), BF)
        scores = dot(queries, keys, 1, 1) + mask_ref[...]
        top = jnp.max(scores, axis=1, keepdims=True)
        weights = jnp.exp(scores - top)
        total = jnp.sum(weights, axis=1, keepdims=True)
        probs = (weights * (1.0 / total)).astype(BF)
        log_ref[0, :, head : head + 1] = top + jnp.log(total)
        heads_ref[0, :, lanes[0]] = dot(probs, values, 1, 0).astype(BF)
    branch = dot(heads_ref[0], weight_ref[3 * width :, :], 1, 0)
    write_halves(branch, rows, keep_ref, other_ref, send_ref)


def attend(place, blocks, near, side, row):
    micro, rows, model = blocks[0].shape
    group = 4 * rows
    width = 2 * (BODY + HALO)
    count = width // HEAD_DIM
    return pl.pallas_call(
        attend_kernel,
        grid=(micro,),
        in_specs=[SCALARS] + [per((rows, model))] * 4
        + [whole(b) for b in near + side] + [per(row.shape[1:])],
        out_specs=[
            per((group, model)), per((group, 3 * width)), per((group, 128)),
            per((group, width)), full((8, model)), full((24, model // 2)),
            per((rows, model)), per((rows, model)), per((2 * rows, model)),
        ],
        out_shape=[
            shape_of(BF, micro, group, model), shape_of(BF, micro, group, 3 * width),
            shape_of(F32, micro, group, 128), shape_of(BF, micro, group, width),
            shape_of(F32, 8, model),
            shape_of(F32, 24, model // 2), shape_of(F32, micro, rows, model),
            shape_of(BF, micro, rows, model), shape_of(BF, micro, 2 * rows, model),
        ],
        scratch_shapes=[
            pltpu.VMEM((4 * width, model), BF), pltpu.VMEM((group, group), F32),
            pltpu.VMEM((1, 3 * width), F32),
        ],
        compiler_params=params(56),
        cost_estimate=pl.CostEstimate(
            flops=2 * micro * group * model * 4 * width,
            bytes_accessed=12 * micro * group * model,
            transcendentals=micro * count * group * group,
        ),
        name="attend",
    )(place, *blocks, *near, *side, row)


def middle_kernel(x_ref, keep_ref, arrived_ref, across_ref, vec_ref, middle_ref, normed_ref):
    rows = x_ref.shape[1]
    branch = keep_ref[0] + arrived_ref[0, :rows, :].astype(F32) + across_ref[0].astype(F32)
    middle = x_ref[0].astype(F32) + branch + vec_ref[4:5, :]
    middle_ref[0] = middle
    hat, _ = norm_stats(middle)
    normed_ref[0] = (hat * vec_ref[5:6, :] + vec_ref[6:7, :]).astype(BF)


def middle_rows(x, keep, arrived, across, vec):
    micro, rows, model = x.shape
    one = per((rows, model))
    return pl.pallas_call(
        middle_kernel,
        grid=(micro,),
        in_specs=[one, one, per((2 * rows, model)), one, whole(vec)],
        out_specs=[one, one],
        out_shape=[shape_of(F32, micro, rows, model), shape_of(BF, micro, rows, model)],
        name="middle_rows",
    )(x, keep, arrived, across, vec)


def stack_parts(parts, refs, low, high, to_ref):
    for (block, start), part_ref in zip(parts, refs):
        first, last = max(start, low), min(start + part_ref.shape[0], high)
        to = block * (high - low) - low
        to_ref[to + first : to + last, :] = part_ref[first - start : last - start, :]


def parts_between(blocks, low, high):
    parts, arrays = [], []
    for block, pieces in enumerate(blocks):
        start = 0
        for piece in pieces:
            if start < high and start + piece.shape[0] > low:
                parts.append((block, start))
                arrays.append(piece)
            start += piece.shape[0]
    return parts, arrays


def pull_kernel(parts, g0, g1, g2, g3, *rest):
    *part_refs, pull_ref, grad_ref, down_ref = rest
    rows = g0.shape[1]
    each = down_ref.shape[0] // 8

    @pl.when(pl.program_id(0) == 0)
    def _():
        stack_parts(parts, part_refs, 0, each, down_ref)

    for i, block_ref in enumerate((g0, g1, g2, g3)):
        grad_ref[i * rows : (i + 1) * rows, :] = block_ref[0]
    pull_ref[0] = dot(grad_ref[...], down_ref[...], 1, 1).astype(BF)


def feed_pull(grads, blocks):
    micro, rows, model = grads[0].shape
    group = 4 * rows
    each = sum(p.shape[0] for p in blocks[0]) // 2
    hidden = 8 * each
    parts, arrays = parts_between(blocks, 0, each)
    return pl.pallas_call(
        partial(pull_kernel, parts),
        grid=(micro,),
        in_specs=[per((rows, model))] * 4 + [whole(b) for b in arrays],
        out_specs=per((group, hidden)),
        out_shape=shape_of(BF, micro, group, hidden),
        scratch_shapes=[pltpu.VMEM((group, model), BF), pltpu.VMEM((hidden, model), BF)],
        compiler_params=params(56),
        cost_estimate=pl.CostEstimate(
            flops=2 * micro * group * model * hidden,
            bytes_accessed=8 * micro * group * model,
            transcendentals=0,
        ),
        name="feed_pull",
    )(*grads, *arrays)


def feed_kernel(parts, x0, x1, x2, x3, pull_ref, bias_ref, *rest):
    *part_refs, active_ref, grad_hidden_ref, keep_ref, other_ref, send_ref, sum_ref, x_ref, up_ref = rest
    rows = x0.shape[1]
    each = up_ref.shape[0] // 8

    @pl.when(pl.program_id(0) == 0)
    def _():
        stack_parts(parts, part_refs, each, 2 * each, up_ref)
        sum_ref[...] = jnp.zeros_like(sum_ref)

    for i, block_ref in enumerate((x0, x1, x2, x3)):
        x_ref[i * rows : (i + 1) * rows, :] = block_ref[0]
    active, slope = gelu_parts(dot(x_ref[...], up_ref[...], 1, 1) + bias_ref[...])
    active_ref[0] = active.astype(BF)
    grad_hidden = (pull_ref[0].astype(F32) * slope).astype(BF)
    grad_hidden_ref[0] = grad_hidden
    sum_ref[...] += jnp.sum(grad_hidden.astype(F32), axis=0, keepdims=True)
    write_halves(dot(grad_hidden, up_ref[...], 1, 0), rows, keep_ref, other_ref, send_ref)


def halves_of(micro, rows, model):
    specs = [per((rows, model)), per((rows, model)), per((2 * rows, model))]
    return specs, [
        shape_of(F32, micro, rows, model), shape_of(BF, micro, rows, model),
        shape_of(BF, micro, 2 * rows, model),
    ]


def feed_forward(x, pull, blocks, bias):
    micro, rows, model = x[0].shape
    group = 4 * rows
    hidden = pull.shape[2]
    specs, shapes = halves_of(micro, rows, model)
    parts, arrays = parts_between(blocks, hidden // 8, hidden // 4)
    return pl.pallas_call(
        partial(feed_kernel, parts),
        grid=(micro,),
        in_specs=[per((rows, model))] * 4 + [per((group, hidden)), whole(bias)]
        + [whole(b) for b in arrays],
        out_specs=[per((group, hidden))] * 2 + specs + [full((1, hidden))],
        out_shape=[shape_of(BF, micro, group, hidden)] * 2 + shapes + [shape_of(F32, 1, hidden)],
        scratch_shapes=[pltpu.VMEM((group, model), BF), pltpu.VMEM((hidden, model), BF)],
        compiler_params=params(56),
        cost_estimate=pl.CostEstimate(
            flops=4 * micro * group * model * hidden,
            bytes_accessed=12 * micro * group * model,
            transcendentals=micro * group * hidden,
        ),
        name="feed_forward",
    )(*x, pull, bias, *arrays)


def feed_out_kernel(parts, active_ref, *rest):
    *part_refs, keep_ref, other_ref, send_ref, down_ref = rest

    @pl.when(pl.program_id(0) == 0)
    def _():
        stack_parts(parts, part_refs, 0, down_ref.shape[0] // 8, down_ref)

    write_halves(
        dot(active_ref[0], down_ref[...], 1, 0), keep_ref.shape[1], keep_ref, other_ref, send_ref
    )


def feed_out(active, blocks):
    micro, group, hidden = active.shape
    parts, arrays = parts_between(blocks, 0, hidden // 8)
    model = arrays[0].shape[1]
    specs, shapes = halves_of(micro, group // 4, model)
    return pl.pallas_call(
        partial(feed_out_kernel, parts),
        grid=(micro,),
        in_specs=[per((group, hidden))] + [whole(b) for b in arrays],
        out_specs=specs,
        out_shape=shapes,
        scratch_shapes=[pltpu.VMEM((hidden, model), BF)],
        compiler_params=params(56),
        cost_estimate=pl.CostEstimate(
            flops=2 * micro * group * model * hidden,
            bytes_accessed=8 * micro * group * model,
            transcendentals=0,
        ),
        name="feed_out",
    )(active, *arrays)


def rows_from(refs, to_ref):
    micro, rows, _ = refs[0].shape
    for m in range(micro):
        for i, block_ref in enumerate(refs):
            at = (4 * m + i) * rows
            to_ref[at : at + rows, :] = block_ref[m]


def feed_grads_kernel(active_ref, grad_hidden_ref, g0, g1, g2, g3, x0, x1, x2, x3, *rest):
    *outs, total_ref, right_ref = rest
    each = outs[0].shape[0] // 2
    step = pl.program_id(0)
    hidden = active_ref.shape[1]
    cut = hidden // 256 * 128
    for left_ref, refs, part in (
        (active_ref, (g0, g1, g2, g3), 0), (grad_hidden_ref, (x0, x1, x2, x3), 1)
    ):

        @pl.when(step == part)
        def _():
            rows_from(refs, right_ref)
            total_ref[:cut, :] = dot(left_ref[:, :cut], right_ref[...], 0, 0)
            total_ref[cut:, :] = dot(left_ref[:, cut:], right_ref[...], 0, 0)
            for i, out_ref in enumerate(outs):
                rows = total_ref[(i + 1) * each : (i + 2) * each, :].astype(BF)
                out_ref[part * each : (part + 1) * each, :] = rows


def feed_grads(active, grad_hidden, grad, x):
    rows, hidden = active.shape
    model = grad[0].shape[2]
    block = (hidden // 4, model)
    arrays = [active, grad_hidden, *grad, *x]
    return pl.pallas_call(
        feed_grads_kernel,
        grid=(2,),
        in_specs=[whole(a) for a in arrays],
        out_specs=[full(block)] * 7,
        out_shape=[shape_of(BF, *block)] * 7,
        scratch_shapes=[pltpu.VMEM((hidden, model), F32), pltpu.VMEM((rows, model), BF)],
        compiler_params=params(56),
        cost_estimate=pl.CostEstimate(
            flops=4 * rows * model * hidden, bytes_accessed=12 * rows * model, transcendentals=0
        ),
        name="feed_grads",
    )(*arrays)


def feed_grads_first_kernel(
    active_ref, grad_hidden_ref, g0, g1, g2, g3, x0, x1, x2, x3, out_ref, total_ref, right_ref
):
    each = out_ref.shape[0] // 2
    step = pl.program_id(0)
    for left_ref, refs, part in (
        (active_ref, (g0, g1, g2, g3), 0), (grad_hidden_ref, (x0, x1, x2, x3), 1)
    ):
        rows_from(refs, right_ref)
        rows = dot(left_ref[...], right_ref[...], 0, 0)[:each]
        at = slice(part * each, (part + 1) * each)

        @pl.when(step == 0)
        def _():
            total_ref[at, :] = rows

        @pl.when(step > 0)
        def _():
            total_ref[at, :] += rows

    @pl.when(step == pl.num_programs(0) - 1)
    def _():
        out_ref[...] = total_ref[...].astype(BF)


def feed_grads_first(active, grad_hidden, grad, x):
    rows, hidden = active.shape
    micro, own, model = grad[0].shape
    group = 4 * own
    block = (hidden // 4, model)
    left = pl.BlockSpec((group, 256), lambda i: (i, 0))
    return pl.pallas_call(
        feed_grads_first_kernel,
        grid=(micro,),
        in_specs=[left] * 2 + [per((own, model))] * 8,
        out_specs=full(block),
        out_shape=shape_of(BF, *block),
        scratch_shapes=[pltpu.VMEM(block, F32), pltpu.VMEM((group, model), BF)],
        compiler_params=params(56),
        cost_estimate=pl.CostEstimate(
            flops=rows * model * hidden // 2, bytes_accessed=8 * rows * model, transcendentals=0
        ),
        name="feed_grads_first",
    )(active, grad_hidden, *grad, *x)


def middle_pull_kernel(
    out_ref, middle_ref, keep_ref, arrived_ref, across_ref, vec_ref, grad_ref, branch_ref, sum_ref
):
    rows = out_ref.shape[1]
    back = keep_ref[0] + arrived_ref[0, :rows, :].astype(F32) + across_ref[0].astype(F32)
    hat, scale = norm_stats(middle_ref[0])
    out = out_ref[0].astype(F32)
    grad = out + norm_pull(back, hat, scale, vec_ref[5:6, :])
    grad_ref[0] = grad
    branch = grad.astype(BF)
    branch_ref[0] = branch

    @pl.when(pl.program_id(0) == 0)
    def _():
        sum_ref[...] = jnp.zeros_like(sum_ref)

    for i, terms in enumerate((branch.astype(F32), back * hat, back, out)):
        sum_ref[i : i + 1, :] += jnp.sum(terms, axis=0, keepdims=True)


def middle_pull(out, middle, keep, arrived, across, vec):
    micro, rows, model = out.shape
    one = per((rows, model))
    return pl.pallas_call(
        middle_pull_kernel,
        grid=(micro,),
        in_specs=[one, one, one, per((2 * rows, model)), one, whole(vec)],
        out_specs=[one, one, full((4, model))],
        out_shape=[
            shape_of(F32, micro, rows, model), shape_of(BF, micro, rows, model),
            shape_of(F32, 4, model),
        ],
        name="middle_pull",
    )(out, middle, keep, arrived, across, vec)


def attend_pull_kernel(
    place_ref, g0, g1, g2, g3, n0, n1, n2, n3, m0, m1, m2, m3, row_ref,
    qkv_ref, log_ref, heads_ref, normed_ref,
    keep_ref, other_ref, send_ref, k0, k1, k2, k3, s0, s1, s2, s3, bias_ref,
    grad_ref, grad_qkv_ref, total_ref, sum_ref, weight_ref, mask_ref,
):
    width = heads_ref.shape[2]
    count = width // HEAD_DIM
    rows = g0.shape[1]
    model = g0.shape[2]
    scale = HEAD_DIM ** (-0.5)
    step = pl.program_id(0)

    @pl.when(step == 0)
    def _():
        assemble(place_ref, (n0, n1, n2, n3), (m0, m1, m2, m3), weight_ref)

    write_mask(row_ref, mask_ref)
    for i, block_ref in enumerate((g0, g1, g2, g3)):
        grad_ref[i * rows : (i + 1) * rows, :] = block_ref[0]
    grad_heads = dot(grad_ref[...], weight_ref[3 * width :, :], 1, 1).astype(BF)
    for head in range(count):
        lanes = [slice(i * width + head * HEAD_DIM, i * width + (head + 1) * HEAD_DIM) for i in range(3)]
        queries, keys, values = [qkv_ref[0, :, part] for part in lanes]
        scores = dot(queries * jnp.asarray(scale, BF), keys, 1, 1) + mask_ref[...]
        probs = jnp.exp(scores - log_ref[0, :, head : head + 1])
        grad = grad_heads[:, lanes[0]]
        delta = jnp.sum(
            grad.astype(F32) * heads_ref[0, :, lanes[0]].astype(F32), axis=1, keepdims=True
        )
        grad_scores = (probs * (dot(grad, values, 1, 1) - delta)).astype(BF)
        grad_qkv_ref[:, lanes[0]] = (scale * dot(grad_scores, keys, 1, 0)).astype(BF)
        grad_qkv_ref[:, lanes[1]] = (scale * dot(grad_scores, queries, 0, 0)).astype(BF)
        grad_qkv_ref[:, lanes[2]] = dot(probs.astype(BF), grad, 0, 0).astype(BF)
    write_halves(dot(grad_qkv_ref[...], weight_ref[: 3 * width, :], 1, 0), rows, keep_ref, other_ref, send_ref)
    qkv_part = dot(grad_qkv_ref[...], normed_ref[0], 0, 0)
    out_part = dot(heads_ref[0], grad_ref[...], 0, 0)
    sums = jnp.sum(grad_qkv_ref[...].astype(F32), axis=0, keepdims=True)

    @pl.when(step == 0)
    def _():
        total_ref[: 3 * width, :] = qkv_part
        total_ref[3 * width :, :] = out_part
        sum_ref[...] = jnp.broadcast_to(sums, sum_ref.shape)

    @pl.when(step > 0)
    def _():
        total_ref[: 3 * width, :] += qkv_part
        total_ref[3 * width :, :] += out_part
        sum_ref[...] += sums

    @pl.when(step == pl.num_programs(0) - 1)
    def _():
        z, y, ctx = place_ref[0], place_ref[1], place_ref[2]
        for k, pair in zip(SHIFTS, ((k0, s0), (k1, s1), (k2, s2), (k3, s3))):
            region = lax.rem(z + 4 - k, 4) * width
            for out_ref, half in zip(pair, (y, 1 - y)):
                start = pl.multiple_of(region + BODY * half, HEAD_DIM)
                out_ref[:BODY, :] = total_ref[pl.ds(start, BODY), :].astype(BF)
                start = pl.multiple_of(region + 2 * BODY + HALO * half, HALO)
                out_ref[BODY:, :] = total_ref[pl.ds(start, HALO), :].astype(BF)
        own = head_places((width, model), 0, ctx)
        hot = (lax.broadcasted_iota(jnp.int32, (width, model), 1) == own).astype(F32)
        for i, part in enumerate((0, 2)):
            line = lax.dot_general(
                sum_ref[:, part * width : (part + 1) * width],
                hot,
                (((1,), (0,)), ((), ())),
                preferred_element_type=F32,
                precision=lax.Precision.HIGHEST,
            )
            bias_ref[i : i + 1, :] = line[0:1]


def attend_pull(place, grads, near, side, row, qkv, log_total, heads, normed):
    micro, rows, model = grads[0].shape
    group = 4 * rows
    width = heads.shape[2]
    count = width // HEAD_DIM
    block = (BODY + HALO, model)
    one = per((rows, model))
    return pl.pallas_call(
        attend_pull_kernel,
        grid=(micro,),
        in_specs=[SCALARS] + [one] * 4 + [whole(b) for b in near + side] + [
            per(row.shape[1:]), per((group, 3 * width)), per((group, 128)),
            per((group, width)), per((group, model)),
        ],
        out_specs=[one, one, per((2 * rows, model))] + [full(block)] * 8 + [full((2, model))],
        out_shape=[
            shape_of(F32, micro, rows, model), shape_of(BF, micro, rows, model),
            shape_of(BF, micro, 2 * rows, model),
        ] + [shape_of(BF, *block)] * 8 + [shape_of(F32, 2, model)],
        scratch_shapes=[
            pltpu.VMEM((group, model), BF), pltpu.VMEM((group, 3 * width), BF),
            pltpu.VMEM((4 * width, model), F32), pltpu.VMEM((8, 3 * width), F32),
            pltpu.VMEM((4 * width, model), BF), pltpu.VMEM((group, group), F32),
        ],
        compiler_params=params(60),
        cost_estimate=pl.CostEstimate(
            flops=2 * micro * group * model * 10 * width,
            bytes_accessed=12 * micro * group * model,
            transcendentals=micro * count * group * group,
        ),
        name="attend_pull",
    )(place, *grads, *near, *side, row, qkv, log_total, heads, normed)


def input_pull_kernel(
    x_ref, grad_ref, keep_ref, arrived_ref, across_ref, vec_ref, out_ref, sum_ref
):
    rows = x_ref.shape[1]
    back = keep_ref[0] + arrived_ref[0, :rows, :].astype(F32) + across_ref[0].astype(F32)
    hat, scale = norm_stats(x_ref[0].astype(F32))
    out = grad_ref[0] + norm_pull(back, hat, scale, vec_ref[0:1, :])
    out_ref[0] = jnp.transpose(out).astype(BF)

    @pl.when(pl.program_id(0) == 0)
    def _():
        sum_ref[...] = jnp.zeros_like(sum_ref)

    for i, terms in enumerate((back * hat, back)):
        sum_ref[i : i + 1, :] += jnp.sum(terms, axis=0, keepdims=True)


def input_pull(x, grad, keep, arrived, across, vec):
    micro, rows, model = x.shape
    one = per((rows, model))
    out, sums = pl.pallas_call(
        input_pull_kernel,
        grid=(micro,),
        in_specs=[one, one, one, per((2 * rows, model)), one, whole(vec)],
        out_specs=[per((model, rows)), full((2, model))],
        out_shape=[shape_of(BF, micro, model, rows), shape_of(F32, 2, model)],
        name="input_pull",
    )(x, grad, keep, arrived, across, vec)
    return out.transpose(0, 2, 1), sums


def mixed_kernel(middle_ref, keep_ref, arrived_ref, across_ref, vec_ref, out_ref):
    rows = middle_ref.shape[1]
    feed = keep_ref[0] + arrived_ref[0, :rows, :].astype(F32) + across_ref[0].astype(F32)
    out_ref[0] = jnp.transpose(middle_ref[0] + feed + vec_ref[7:8, :]).astype(BF)


def mixed_rows(middle, keep, arrived, across, vec):
    micro, rows, model = middle.shape
    one = per((rows, model))
    return pl.pallas_call(
        mixed_kernel,
        grid=(micro,),
        in_specs=[one, one, per((2 * rows, model)), one, whole(vec)],
        out_specs=per((model, rows)),
        out_shape=shape_of(BF, micro, model, rows),
        name="mixed_rows",
    )(middle, keep, arrived, across, vec).transpose(0, 2, 1)


def row_places(segments, rows):
    ctx = lax.axis_index("ctx")
    ranks = [ctx ^ j for j in BLOCKS]
    starts = segments[:, 0].reshape(-1, 4, rows).transpose(1, 0, 2)
    starts = jnp.concatenate([pick(starts, r) for r in ranks], axis=1)
    places = jnp.concatenate([r * rows + jnp.arange(rows, dtype=jnp.int32) for r in ranks])
    places = jnp.broadcast_to(places[None], starts.shape)
    return jnp.stack([starts, places] + [places] * 6, axis=1)


def own_up_bias(lines, order, width):
    table = lines[16:].reshape(order.shape[0], 4, width).transpose(1, 0, 2)
    return reorder(pick(table, lax.axis_index("ctx")), order).reshape(1, -1)


def vector_parts(first_sums, bias_sums, sums, up_sum, order, width):
    up_rows = reorder_back(up_sum.reshape(order.shape[0], width), order)
    mine = (jnp.arange(4) == lax.axis_index("ctx")).astype(F32)
    table = jnp.concatenate([first_sums, bias_sums, sums], axis=0)
    up_part = (up_rows[:, None, :] * mine[None, :, None]).reshape(-1)
    return jnp.concatenate([table.reshape(-1), up_part])


def flat(values):
    return values.reshape(-1, values.shape[-1])


def halo_pairs(back):
    pairs = []
    for p in range(8):
        for c in range(4):
            to = (c - 1) % 4 if (p % 2 == 1) != back else (c + 1) % 4
            pairs.append((p * 4 + c, p * 4 + to))
    return pairs


def aligned_block(w_attn, vectors, odd, ctx):
    turned = row_major(w_attn.T)
    width, model = turned.shape
    table = ctx_table(vectors, ctx).astype(BF).reshape(3, model // 2)
    edge = jnp.where(odd, turned[:HALO], turned[width - HALO :])
    halo = lax.ppermute(edge, BOTH, halo_pairs(False))
    none = jnp.zeros_like(halo)
    wide = jnp.concatenate(
        [jnp.where(odd, none, halo), turned, jnp.where(odd, halo, none)], axis=0
    )
    shift = HALO * odd.astype(jnp.int32)
    body = lax.dynamic_slice_in_dim(wide, HALO - 8 * ctx + shift, BODY, axis=0)
    extra = lax.dynamic_slice_in_dim(wide, width + shift, HALO, axis=0)
    extra = jnp.where(ctx == 3, extra, jnp.zeros_like(extra))
    lines = jnp.pad(table, ((0, 13), (0, model // 2)))
    return jnp.concatenate([body, extra, lines], axis=0)


def aligned_owned(own, odd, ctx, width):
    last = ctx == 3
    body, extra = own[:BODY], own[BODY:]
    tail = jnp.where(last, extra, body[BODY - HALO :])
    halo = lax.ppermute(jnp.where(odd, tail, body[:HALO]), BOTH, halo_pairs(True))
    halo = jnp.where(last & jnp.logical_not(odd), extra, halo)
    wide = jnp.where(
        odd, jnp.concatenate([halo, body], axis=0), jnp.concatenate([body, halo], axis=0)
    )
    return lax.dynamic_slice_in_dim(wide, 8 * ctx, width, axis=0)


def vector_sides(part, y, ctx):
    table = part.reshape(8, 4, -1).transpose(1, 0, 2)
    mine = jnp.stack([pick(table, ctx ^ j) for j in (0, 1)])
    far = jnp.stack([pick(table, ctx ^ j) for j in (2, 3)])
    mine = mine + lax.ppermute(far, "ctx", CHIP_PAIRS)
    mine = mine[0] + lax.ppermute(mine[1], "ctx", CORE_PAIRS)
    sides = mine.reshape(4, 2, -1).transpose(1, 0, 2)
    return pick(sides, y) + lax.ppermute(pick(sides, 1 - y), "dp", SIDE_PAIRS)


def vector_owned(mine, z):
    total = pick(mine, z)
    for k in (1, 2, 3):
        total = total + to_shift(pick(mine, (z - k) % 4)[None], k, True)[0]
    return total


def both(keep, arrived):
    return keep.astype(F32) + arrived.astype(F32)


def aligned(tokens, cotangent, w_attn, w_up, w_down, vectors, segments):
    rows = tokens.shape[1]
    width = w_attn.shape[1]
    ctx, dp = lax.axis_index("ctx"), lax.axis_index("dp")
    z, y = dp // 2, dp % 2
    odd = y == 1
    place = jnp.stack([z, y, ctx]).astype(jnp.int32)
    order = jnp.stack(dp_order(z, y))
    tokens, cotangent = row_major(tokens), row_major(cotangent)
    row_info = row_places(segments, rows)
    feed = jnp.concatenate([w_down, w_up.T], axis=0)

    n0 = aligned_block(w_attn, vectors, odd, ctx)
    n0, t0, place, row_info, b0 = hold([n0, tokens, place, row_info, feed])
    n1, n3, s0, t1, c0 = (
        to_shift(n0, 1), to_shift(n0, 3), to_side(n0), to_chip(t0), to_side(b0[:CUT])
    )
    n0, n1, n3, s0, t0, t1, g0, b0, c0 = hold([n0, n1, n3, s0, t0, t1, cotangent, b0, c0])
    n2, s1, s3, g1 = to_shift(n0, 2), to_side(n1), to_side(n3), to_chip(g0)
    n0, n1, n2, n3, s0, s1, s3, t0, t1, g0, g1, b0 = hold(
        [n0, n1, n2, n3, s0, s1, s3, t0, t1, g0, g1, b0]
    )
    s2, b1, t2, t3 = to_side(n2), to_shift(b0, 1), to_core(t0), to_core(t1)
    n0, n1, n2, n3, s0, s1, s2, s3, t0, t1, t2, t3, g0, g1, b0, b1 = hold(
        [n0, n1, n2, n3, s0, s1, s2, s3, t0, t1, t2, t3, g0, g1, b0, b1]
    )
    b3, b2, c1 = to_shift(b0, 3), to_shift(b0[: THIRDS[0]], 2), to_side(b1)
    g2, g3 = to_core(g0), to_core(g1)
    normed_one, qkv, log_total, heads, lines, rest, keep, other, away = attend(
        place, [t0, t1, t2, t3], [n0, n1, n3, n2], [s0, s1, s3, s2], row_info
    )
    away, keep, other, b0, b1, b2, b3, c1, g0, g1, g2, g3 = hold(
        [away, keep, other, b0, b1, b2, b3, c1, g0, g1, g2, g3]
    )
    arrived = to_core(away)
    away, arrived, keep, b0, b2, b3 = hold([half_sum(other, arrived), arrived, keep, b0, b2, b3])
    across, d2, c3, c2 = (
        to_chip(away), to_shift(b0[THIRDS[0] : THIRDS[1]], 2), to_side(b3), to_side(b2)
    )
    across, arrived, keep, b0, d2, c3, c2 = hold([across, arrived, keep, b0, d2, c3, c2])
    middle, h0 = middle_rows(tokens, keep, arrived, across, lines)
    h0, middle, b0, d2 = hold([h0, middle, b0, d2])
    h1, h2, e2, f2 = to_chip(h0), to_core(h0), to_shift(b0[THIRDS[1] :], 2), to_side(d2)
    d0 = to_side(b0[CUT:])
    up_bias = own_up_bias(rest, order, width)
    h0, h1, h2, e2, f2, d0, up_bias = hold([h0, h1, h2, e2, f2, d0, up_bias])
    h3, a2 = to_core(h1), to_side(e2)
    blocks = [[c2, f2, a2], [b2, d2, e2], [b0], [c0, d0], [b1], [c1], [b3], [c3]]
    pull = feed_pull([g0, g1, g2, g3], blocks)
    h0, h1, h2, h3, pull = hold([h0, h1, h2, h3, pull], a2)
    active, grad_hidden, keep, other, away, up_sum = feed_forward(
        [h0, h1, h2, h3], pull, blocks, up_bias
    )
    x_all, grad_all = [h0, h1, h2, h3], [g0, g1, g2, g3]

    arrived = to_core(away)
    q2 = feed_grads_first(flat(active), flat(grad_hidden), grad_all, x_all)
    away, arrived, keep, active, q2 = hold(
        [half_sum(other, arrived), arrived, keep, active, q2]
    )
    across, q2 = to_chip(away), to_side(q2)
    p2, p0, q0, p1, q1, p3, q3 = feed_grads(flat(active), flat(grad_hidden), grad_all, x_all)
    across, arrived, keep, p2, q2 = hold([across, arrived, keep, p2, q2])
    grad_middle, h0, sums = middle_pull(cotangent, middle, keep, arrived, across, lines)
    h0, p2, q3, grad_middle, active = hold([h0, both(p2, q2).astype(BF), q3, grad_middle, active])
    h1, h2, r2, q3 = to_chip(h0), to_core(h0), to_shift(p2[:BACK_CUT], 2, True), to_side(q3)
    feed_keep, feed_other, feed_away = feed_out(active, blocks)
    h0, h1, h2, r2, q3, p2, feed_away = hold([h0, h1, h2, r2, q3, p2, feed_away])
    h3, feed_arrived = to_core(h1), to_core(feed_away)
    h0, h1, h2, h3, p2, p3, q1, q0, feed_arrived = hold(
        [h0, h1, h2, h3, p2, both(p3, q3).astype(BF), q1, q0, feed_arrived]
    )
    t2, r3 = to_shift(p2[BACK_CUT:], 2, True), to_shift(p3, 3, True)
    q1, q0 = to_side(q1), to_side(q0)
    keep, other, away, *parts, bias_sums = attend_pull(
        place, [h0, h1, h2, h3], [n0, n1, n3, n2], [s0, s1, s3, s2], row_info,
        qkv, log_total, heads, normed_one,
    )
    away, t2, r3, q1, q0, p0, p1, *parts = hold([away, t2, r3, q1, q0, p0, p1] + parts)
    k0, k1, k3, k2, l0, l1, l3, l2 = parts
    arrived = to_core(away)
    away, arrived, keep, p1, l1, l2, l3 = hold(
        [half_sum(other, arrived), arrived, keep, both(p1, q1).astype(BF), l1, l2, l3]
    )
    r1, across, l2, l1 = to_shift(p1, 1, True), to_chip(away), to_side(l2), to_side(l1)
    across, arrived, keep, r1, k1, k2, l0, l3, feed_away = hold(
        [
            across, arrived, keep, r1, both(k1, l1).astype(BF), both(k2, l2).astype(BF),
            l0, l3, half_sum(feed_other, feed_arrived),
        ]
    )
    k2, k1, l3, l0, feed_across = (
        to_shift(k2, 2, True), to_shift(k1, 1, True), to_side(l3), to_side(l0),
        to_chip(feed_away),
    )
    input_grad, first_sums = input_pull(tokens, grad_middle, keep, arrived, across, lines)
    part = vector_parts(first_sums, bias_sums, sums, up_sum, order, width)
    k1, k2, k3, l0, part, feed_across, input_grad = hold(
        [k1, k2, both(k3, l3).astype(BF), l0, part, feed_across, input_grad]
    )
    k3, part = to_shift(k3, 3, True), vector_sides(part, y, ctx)
    mixed = mixed_rows(middle, feed_keep, feed_arrived, feed_across, lines)
    terms = [p0, q0, r1, jnp.concatenate([r2, t2], axis=0), r3]
    down_owned = sum(t[:width].astype(F32) for t in terms)
    up_owned = sum(t[width:].astype(F32) for t in terms).T
    k3, part, mixed, down_owned, up_owned = hold([k3, part, mixed, down_owned, up_owned])
    own = both(k0, l0) + k1.astype(F32) + k2.astype(F32) + k3.astype(F32)
    attn_owned = aligned_owned(own, odd, ctx, width)
    return (
        mixed, input_grad, attn_owned.T, up_owned, down_owned, vector_owned(part, z),
    )


def plain(tokens, cotangent, w_attn, w_up, w_down, vectors, segments):
    micro, rows, model = tokens.shape
    width = w_attn.shape[1]
    ctx = lax.axis_index("ctx")
    last = ctx == lax.axis_size("ctx") - 1
    place = jnp.stack([jnp.zeros((), ctx.dtype), jnp.zeros((), ctx.dtype), ctx])
    order = jnp.arange(lax.axis_size("dp"))
    table = lax.all_gather(w_attn.T, BOTH, axis=0, tiled=True)
    lines = lax.all_gather(vectors, BOTH, axis=0, tiled=True).reshape(24, model // 2)
    lines = jnp.pad(lines, ((0, 0), (0, model // 2)))
    near, side = [], []
    for region in (-k % 4 for k in SHIFTS):
        part = head_rows(table[region * model : (region + 1) * model], ctx, last)
        for blocks, half in ((near, 0), (side, 1)):
            line = 3 * (2 * region + half)
            blocks.append(
                jnp.concatenate(
                    [
                        part[BODY * half : BODY * (half + 1)],
                        part[2 * BODY + HALO * half : 2 * BODY + HALO * (half + 1)],
                        jnp.pad(lines[line : line + 3], ((0, 13), (0, 0))),
                    ],
                    axis=0,
                )
            )
    up = lax.all_gather(w_up.T, "dp", axis=0, tiled=True)
    down = lax.all_gather(w_down, "dp", axis=0, tiled=True)
    each = up.shape[0] // 8
    blocks = [
        jnp.concatenate([w[i * each : (i + 1) * each] for w in (down, up)], axis=0)
        for i in range(8)
    ]
    blocks = [[b] for b in blocks]
    row_info = row_places(segments, rows)

    normed_one, qkv, log_total, heads, lines, rest, *halves = attend(
        place, row_gather(tokens), near, side, row_info
    )
    middle, normed_two = middle_rows(tokens, *row_scatter(*halves), lines)
    x_all, grad_all = row_gather(normed_two), row_gather(cotangent)
    active, grad_hidden, *halves, up_sum = feed_forward(
        x_all, feed_pull(grad_all, blocks), blocks, own_up_bias(rest, order, width)
    )
    mixed = mixed_rows(middle, *row_scatter(*feed_out(active, blocks)), lines)
    grad_middle, branch, sums = middle_pull(cotangent, middle, *row_scatter(*halves), lines)
    arrays = flat(active), flat(grad_hidden), grad_all, x_all
    parts = [feed_grads_first(*arrays)] + list(feed_grads(*arrays))
    down_owned, up_owned = [
        lax.psum_scatter(
            jnp.concatenate([p[i * each : (i + 1) * each] for p in parts], axis=0),
            "dp", scatter_dimension=0, tiled=True,
        ).astype(F32)
        for i in range(2)
    ]
    *halves, k0, k1, k2, k3, s0, s1, s2, s3, bias_sums = attend_pull(
        place, row_gather(branch), near, side, row_info, qkv, log_total, heads, normed_one
    )
    input_grad, first_sums = input_pull(tokens, grad_middle, *row_scatter(*halves), lines)
    parts = []
    for region in range(4):
        at = SHIFTS.index(-region % 4)
        first, second = (k0, k1, k2, k3)[at], (s0, s1, s2, s3)[at]
        part = [first[:BODY], second[:BODY], first[BODY:], second[BODY:]]
        parts.append(head_rows_back(jnp.concatenate(part, axis=0), ctx, last))
    attn_owned = lax.psum_scatter(
        jnp.concatenate(parts, axis=0), BOTH, scatter_dimension=0, tiled=True
    ).astype(F32)
    part = vector_parts(first_sums, bias_sums, sums, up_sum, order, width)
    vector_grad = lax.psum_scatter(part, BOTH, scatter_dimension=0, tiled=True)
    return (mixed, input_grad, attn_owned.T, up_owned.T, down_owned, vector_grad)


def shards(*arrays):
    fits = lax.axis_size("dp") == 8 and lax.axis_size("ctx") == 4
    return (aligned if fits and arrays[2].shape == (1088, 136) else plain)(*arrays)


def solution(mesh):
    return jax.shard_map(
        shards,
        mesh=mesh,
        in_specs=(
            P(None, BOTH, None),
            P(None, BOTH, None),
            P(None, BOTH),
            P(None, BOTH),
            P(BOTH, None),
            P(BOTH),
            P(None, "dp", None),
        ),
        out_specs=(
            P(None, BOTH, None),
            P(None, BOTH, None),
            P(None, BOTH),
            P(None, BOTH),
            P(BOTH, None),
            P(BOTH),
        ),
        check_vma=False,
    )
```

profile of v0, /device:TPU:0, one launch (start us, length us, event | category | flops | bytes accessed | tf_op | source)
XLA Modules:
  0.0 323.5 jit_solution(13681982135482366252)
XLA Ops:
  17.5 15.3 %collective-permute-done.7 = bf16[9,16,1088]{2,1,0:T(8,128)(2,1)} collective-permute-done((bf16[9,16,1088]{2,1,0:T(8,128)(2,1)S(1)}, bf16[9,16,1088]{2,1,0:T(8,128)(2,1)}, u32[]{:S(2)}, u32[]{:S(2)}) %collective-permute-start.7) | collective-permute-done | bytes 313376 | tf_op jit(solution)/shard_map/ppermute | solution.py:61
  36.3 16.6 %collective-permute-done.8 = bf16[11,16,1088]{2,1,0:T(8,128)(2,1)S(1)} collective-permute-done((bf16[11,16,1088]{2,1,0:T(8,128)(2,1)S(1)}, bf16[11,16,1088]{2,1,0:T(8,128)(2,1)S(1)}, u32[]{:S(2)}, u32[]{:S(2)}) %collective-permute-start.8) | collective-permute-done | bytes 383008 | tf_op jit(solution)/shard_map/ppermute | solution.py:61
  56.1 9.9 %collective-permute-done.12 = bf16[11,16,1088]{2,1,0:T(8,128)(2,1)S(1)} collective-permute-done((bf16[11,16,1088]{2,1,0:T(8,128)(2,1)S(1)}, bf16[11,16,1088]{2,1,0:T(8,128)(2,1)S(1)}, u32[]{:S(2)}, u32[]{:S(2)}) %collective-permute-start.12) | collective-permute-done | bytes 383008 | tf_op jit(solution)/shard_map/ppermute | solution.py:61
  65.9 3.7 %collective-permute-done.15 = bf16[17,16,1088]{2,1,0:T(8,128)(2,1)S(1)} collective-permute-done((bf16[17,16,1088]{2,1,0:T(8,128)(2,1)S(1)}, bf16[17,16,1088]{2,1,0:T(8,128)(2,1)S(1)}, u32[]{:S(2)}, u32[]{:S(2)}) %collective-permute-start.15) | collective-permute-done | bytes 591904 | tf_op jit(solution)/shard_map/ppermute | solution.py:61
  72.9 15.8 %attend.1 = (bf16[2,512,1088]{2,1,0:T(8,128)(2,1)}, bf16[2,512,960]{2,1,0:T(8,128)(2,1)}, f32[2,512,128]{2,1,0:T(8,128)}, bf16[2,512,320]{2,1,0:T(8,128)(2,1)}, ...) custom-call(s32[3]{0:T(128)} %pad_add_fusion.3.place_ref, ...), custom_call_target="tpu_custom_call" | custom-call | flops 2852126720 | bytes 13369344 | tf_op jit(solution)/shard_map/attend/pallas_call | solution.py:272
  90.2 3.1 collective-permute-done.21
  101.0 13.3 %collective-permute-done.25 = bf16[4,16,1088]{2,1,0:T(8,128)(2,1)S(1)} collective-permute-done((bf16[4,16,1088]{2,1,0:T(8,128)(2,1)S(1)}, bf16[4,16,1088]{2,1,0:T(8,128)(2,1)S(1)}, u32[]{:S(2)}, u32[]{:S(2)}) %collective-permute-start.25) | collective-permute-done | bytes 139296 | tf_op jit(solution)/shard_map/ppermute | solution.py:61
  115.2 3.3 %middle_rows.1 = (f32[2,128,1088]{2,1,0:T(8,128)}, bf16[2,128,1088]{2,1,0:T(8,128)(2,1)}) custom-call(bf16[2,128,1088]{2,1,0:T(8,128)(2,1)} %copy-done.2, f32[2,128,1088]{2,1,0:T(8,128)} %get-tuple-element.263.keep_ref, bf16[2,256,1088]{2,1,0:T(8,128)(2,1)} %bitcast.189, bf16[2,128,1088]{2,1,0:T(8,128)(2,1)} %bitcast.232, f32[8,1088]{1,0:T(8,128)} %get-tuple-element.266.vec_ref), custom_call_target="tpu_custom_call" | custom-call | tf_op jit(solution)/shard_map/middle_rows/pallas_call | solution.py:315
  126.5 10.1 %collective-permute-done.29 = bf16[6,16,1088]{2,1,0:T(8,128)(2,1)S(1)} collective-permute-done((bf16[6,16,1088]{2,1,0:T(8,128)(2,1)S(1)}, bf16[6,16,1088]{2,1,0:T(8,128)(2,1)S(1)}, u32[]{:S(2)}, u32[]{:S(2)}) %collective-permute-start.29) | collective-permute-done | bytes 208928 | tf_op jit(solution)/shard_map/ppermute | solution.py:61
  137.3 7.7 %feed_pull.1.pull_ref = bf16[2,512,1088]{2,1,0:T(8,128)(2,1)} custom-call(bf16[2,128,1088]{2,1,0:T(8,128)(2,1)} %copy-done.1, bf16[2,128,1088]{2,1,0:T(8,128)(2,1)} %bitcast.205, bf16[2,128,1088]{2,1,0:T(8,128)(2,1)} %bitcast.208, bf16[2,128,1088]{2,1,0:T(8,128)(2,1)} %bitcast.211, bf16[64,1088]{1,0:T(8,128)(2,1)} %bitcast.307, bf16[96,1088]{1,0:T(8,128)(2,1)} %bitcast.302, ...), custom_call_target="tpu_custom_call" | custom-call | flops 2424307712 | bytes 8912896 | tf_op jit(solution)/shard_map/feed_pull/pallas_call | solution.py:364
  146.3 14.4 %feed_forward.1 = (bf16[2,512,1088]{2,1,0:T(8,128)(2,1)}, bf16[2,512,1088]{2,1,0:T(8,128)(2,1)}, f32[2,128,1088]{2,1,0:T(8,128)}, bf16[2,128,1088]{2,1,0:T(8,128...) custom-call(bf16[2,128,1088]{2,1,0:T(8,128)(2,1)} %get-tuple-element.290.x0, bf16[2,128,1088]{2,1,0:T(8,128)(2,1)} %bitcast.216, ...), custom_call_target="tpu_custom_call" | custom-call | flops 4848615424 | bytes 13369344 | tf_op jit(solution)/shard_map/feed_forward/pallas_call | solution.py:415
  160.9 5.1 %feed_grads_first.1 = bf16[272,1088]{1,0:T(8,128)(2,1)} custom-call(bf16[1024,1088]{1,0:T(8,128)(2,1)} %bitcast.190, bf16[1024,1088]{1,0:T(8,128)(2,1)} %bitcast.192, bf16[2,128,1088]{2,1,0:T(8,128)(2,1)} %copy-done.1, bf16[2,128,1088]{2,1,0:T(8,128)(2,1)} %bitcast.206, bf16[2,128,1088]{2,1,0:T(8,128)(2,1)} %bitcast.209, bf16[2,128,1088]{2,1,0:T(8,128)(2,1)} %bitcast.212, ...), custom_call_target="tpu_custom_call" | custom-call | flops 606076928 | bytes 8912896 | tf_op jit(solution)/shard_map/feed_grads_first/pallas_call | solution.py:546
  169.1 12.3 %feed_grads.1 = (bf16[272,1088]{1,0:T(8,128)(2,1)}, bf16[272,1088]{1,0:T(8,128)(2,1)}, bf16[272,1088]{1,0:T(8,128)(2,1)}, bf16[272,1088]{1,0:T(8,128)(2,1)}, bf1...) custom-call(bf16[1024,1088]{1,0:T(8,128)(2,1)} %bitcast.191, ...), custom_call_target="tpu_custom_call" | custom-call | flops 4848615424 | bytes 13369344 | tf_op jit(solution)/shard_map/feed_grads/pallas_call | solution.py:500
  185.5 4.1 %middle_pull.1 = (f32[2,128,1088]{2,1,0:T(8,128)}, bf16[2,128,1088]{2,1,0:T(8,128)(2,1)}, f32[4,1088]{1,0:T(4,128)}) custom-call(bf16[2,128,1088]{2,1,0:T(8,128)(2,1)} %copy-done.1, f32[2,128,1088]{2,1,0:T(8,128)} %get-tuple-element.271.middle_ref, f32[2,128,1088]{2,1,0:T(8,128)} %get-tuple-element.308.keep_ref, bf16[2,256,1088]{2,1,0:T(8,128)(2,1)} %bitcast.187, ...), custom_call_target="tpu_custom_call" | custom-call | tf_op jit(solution)/shard_map/middle_pull/pallas_call | solution.py:584
  192.2 7.9 %feed_out.1 = (f32[2,128,1088]{2,1,0:T(8,128)}, bf16[2,128,1088]{2,1,0:T(8,128)(2,1)}, bf16[2,256,1088]{2,1,0:T(8,128)(2,1)}) custom-call(bf16[2,512,1088]{2,1,0:T(8,128)(2,1)} %get-tuple-element.319.active_ref, bf16[64,1088]{1,0:T(8,128)(2,1)} %bitcast.308, bf16[96,1088]{1,0:T(8,128)(2,1)} %bitcast.304, bf16[64,1088]{1,0:T(8,128)(2,1)} %bitcast.306, ...), custom_call_target="tpu_custom_call" | custom-call | flops 2424307712 | bytes 8912896 | tf_op jit(solution)/shard_map/feed_out/pallas_call | solution.py:450
  200.2 5.9 %collective-permute-done.38 = bf16[7,16,1088]{2,1,0:T(8,128)(2,1)S(1)} collective-permute-done((bf16[7,16,1088]{2,1,0:T(8,128)(2,1)S(1)}, bf16[7,16,1088]{2,1,0:T(8,128)(2,1)S(1)}, u32[]{:S(2)}, u32[]{:S(2)}) %collective-permute-start.38) | collective-permute-done | bytes 243744 | tf_op jit(solution)/shard_map/ppermute | solution.py:61
  215.7 29.2 %attend_pull.1 = (f32[2,128,1088]{2,1,0:T(8,128)}, bf16[2,128,1088]{2,1,0:T(8,128)(2,1)}, bf16[2,256,1088]{2,1,0:T(8,128)(2,1)}, bf16[160,1088]{1,0:T(8,128)(2,1...) custom-call(s32[3]{0:T(128)} %pad_add_fusion.3.place_ref, ...), custom_call_target="tpu_custom_call" | custom-call | flops 7130316800 | bytes 13369344 | tf_op jit(solution)/shard_map/attend_pull/pallas_call | solution.py:678
  255.3 5.5 %collective-permute-done.49 = bf16[10,16,1088]{2,1,0:T(8,128)(2,1)S(1)} collective-permute-done((bf16[10,16,1088]{2,1,0:T(8,128)(2,1)S(1)}, bf16[10,16,1088]{2,1,0:T(8,128)(2,1)S(1)}, u32[]{:S(2)}, u32[]{:S(2)}) %collective-permute-start.49) | collective-permute-done | bytes 348192 | tf_op jit(solution)/shard_map/ppermute | solution.py:61
  261.6 6.7 %collective-permute-done.50 = bf16[10,16,1088]{2,1,0:T(8,128)(2,1)S(1)} collective-permute-done((bf16[10,16,1088]{2,1,0:T(8,128)(2,1)S(1)}, bf16[10,16,1088]{2,1,0:T(8,128)(2,1)S(1)}, u32[]{:S(2)}, u32[]{:S(2)}) %collective-permute-start.50) | collective-permute-done | bytes 348192 | tf_op jit(solution)/shard_map/ppermute | solution.py:61
  274.2 3.9 %input_pull.1 = (bf16[2,1088,128]{2,1,0:T(8,128)(2,1)}, f32[2,1088]{1,0:T(2,128)}) custom-call(bf16[2,128,1088]{2,1,0:T(8,128)(2,1)} %copy-done.2, f32[2,128,1088]{2,1,0:T(8,128)} %get-tuple-element.378.grad_ref, f32[2,128,1088]{2,1,0:T(8,128)} %get-tuple-element.379.keep_ref, bf16[2,256,1088]{2,1,0:T(8,128)(2,1)} %bitcast.185, ...), custom_call_target="tpu_custom_call" | custom-call | tf_op jit(solution)/shard_map/input_pull/pallas_call | solution.py:725
  280.8 3.2 collective-permute-done.53
  285.9 9.9 %collective-permute-done.52 = bf16[10,16,1088]{2,1,0:T(8,128)(2,1)} collective-permute-done((bf16[10,16,1088]{2,1,0:T(8,128)(2,1)}, bf16[10,16,1088]{2,1,0:T(8,128)(2,1)}, u32[]{:S(2)}, u32[]{:S(2)}) %collective-permute-start.52) | collective-permute-done | bytes 348192 | tf_op jit(solution)/shard_map/ppermute | solution.py:61
  305.8 3.1 mixed_rows.1
  308.9 5.1 %collective-permute-done.56 = bf16[10,16,1088]{2,1,0:T(8,128)(2,1)S(1)} collective-permute-done((bf16[10,16,1088]{2,1,0:T(8,128)(2,1)}, bf16[10,16,1088]{2,1,0:T(8,128)(2,1)S(1)}, u32[]{:S(2)}, u32[]{:S(2)}) %collective-permute-start.56) | collective-permute-done | bytes 348192 | tf_op jit(solution)/shard_map/ppermute | solution.py:61
  (322 shorter events, 106.8 us)
Async XLA Ops:
  9.3 23.5 %collective-permute-start.6 = (bf16[2,8,16,1088]{3,2,1,0:T(8,128)(2,1)S(1)}, bf16[2,8,16,1088]{3,2,1,0:T(8,128)(2,1)}, u32[]{:S(2)}, u32[]{:S(2)}) collective-permute-start(bf16[2,8,16,1088]{3,2,1,0:T(8,128)(2,1)S(1)} %bitcast.180), channel_id=1, source_target_pairs={{0,2},{2,0},{1,3},{3,1},{4,6},{6,4},{5,7},{7,5},{8,10},{10,8},{9,1... | collective-permute-start | bytes 1671176 | tf_op jit(solution)/shard_map/ppermute | solution.py:61
  11.2 21.6 %collective-permute-start.3 = (bf16[11,16,1088]{2,1,0:T(8,128)(2,1)S(1)}, bf16[11,16,1088]{2,1,0:T(8,128)(2,1)}, u32[]{:S(2)}, u32[]{:S(2)}) collective-permute-start(bf16[11,16,1088]{2,1,0:T(8,128)(2,1)S(1)} %bitcast.234), channel_id=1, source_target_pairs={{0,8},{4,12},{8,16},{12,20},{16,24},{20,28},{24,0},{28,4},{1,9},{5... | collective-permute-start | bytes 1148936 | tf_op jit(solution)/shard_map/ppermute | solution.py:61
  12.8 20.0 %collective-permute-start.4 = (bf16[11,16,1088]{2,1,0:T(8,128)(2,1)S(1)}, bf16[11,16,1088]{2,1,0:T(8,128)(2,1)}, u32[]{:S(2)}, u32[]{:S(2)}) collective-permute-start(bf16[11,16,1088]{2,1,0:T(8,128)(2,1)S(1)} %bitcast.235), channel_id=1, source_target_pairs={{0,24},{4,28},{8,0},{12,4},{16,8},{20,12},{24,16},{28,20},{1,25},{... | collective-permute-start | bytes 1148936 | tf_op jit(solution)/shard_map/ppermute | solution.py:61
  15.1 17.7 %collective-permute-start.5 = (bf16[11,16,1088]{2,1,0:T(8,128)(2,1)S(1)}, bf16[11,16,1088]{2,1,0:T(8,128)(2,1)}, u32[]{:S(2)}, u32[]{:S(2)}) collective-permute-start(bf16[11,16,1088]{2,1,0:T(8,128)(2,1)S(1)} %bitcast.236), channel_id=1, source_target_pairs={{0,4},{4,0},{8,12},{12,8},{16,20},{20,16},{24,28},{28,24},{1,5},{5... | collective-permute-start | bytes 1148936 | tf_op jit(solution)/shard_map/ppermute | solution.py:61
  15.7 17.1 %collective-permute-start.7 = (bf16[9,16,1088]{2,1,0:T(8,128)(2,1)S(1)}, bf16[9,16,1088]{2,1,0:T(8,128)(2,1)}, u32[]{:S(2)}, u32[]{:S(2)}) collective-permute-start(bf16[9,16,1088]{2,1,0:T(8,128)(2,1)S(1)} %bitcast.241), channel_id=1, source_target_pairs={{0,4},{4,0},{8,12},{12,8},{16,20},{20,16},{24,28},{28,24},{1,5},{5... | collective-permute-start | bytes 940040 | tf_op jit(solution)/shard_map/ppermute | solution.py:61
  32.8 20.1 %collective-permute-start.11 = (bf16[2,8,16,1088]{3,2,1,0:T(8,128)(2,1)S(1)}, bf16[2,8,16,1088]{3,2,1,0:T(8,128)(2,1)S(1)}, u32[]{:S(2)}, u32[]{:S(2)}) collective-permute-start(bf16[2,8,16,1088]{3,2,1,0:T(8,128)(2,1)S(1)} %bitcast.178), channel_id=1, source_target_pairs={{0,2},{2,0},{1,3},{3,1},{4,6},{6,4},{5,7},{7,5},{8,10},{10,8},{9,1... | collective-permute-start | bytes 1671176 | tf_op jit(solution)/shard_map/ppermute | solution.py:61
  33.4 19.4 %collective-permute-start.8 = (bf16[11,16,1088]{2,1,0:T(8,128)(2,1)S(1)}, bf16[11,16,1088]{2,1,0:T(8,128)(2,1)S(1)}, u32[]{:S(2)}, u32[]{:S(2)}) collective-permute-start(bf16[11,16,1088]{2,1,0:T(8,128)(2,1)S(1)} %bitcast.237), channel_id=1, source_target_pairs={{0,16},{4,20},{8,24},{12,28},{16,0},{20,4},{24,8},{28,12},{1,17},{... | collective-permute-start | bytes 1148936 | tf_op jit(solution)/shard_map/ppermute | solution.py:61
  34.3 18.6 %collective-permute-start.9 = (bf16[11,16,1088]{2,1,0:T(8,128)(2,1)}, bf16[11,16,1088]{2,1,0:T(8,128)(2,1)S(1)}, u32[]{:S(2)}, u32[]{:S(2)}) collective-permute-start(bf16[11,16,1088]{2,1,0:T(8,128)(2,1)} %bitcast.23), channel_id=1, source_target_pairs={{0,4},{4,0},{8,12},{12,8},{16,20},{20,16},{24,28},{28,24},{1,5},{5... | collective-permute-start | bytes 1148936 | tf_op jit(solution)/shard_map/ppermute | solution.py:61
  35.7 17.2 %collective-permute-start.10 = (bf16[11,16,1088]{2,1,0:T(8,128)(2,1)}, bf16[11,16,1088]{2,1,0:T(8,128)(2,1)S(1)}, u32[]{:S(2)}, u32[]{:S(2)}) collective-permute-start(bf16[11,16,1088]{2,1,0:T(8,128)(2,1)} %bitcast.25), channel_id=1, source_target_pairs={{0,4},{4,0},{8,12},{12,8},{16,20},{20,16},{24,28},{28,24},{1,5},{5... | collective-permute-start | bytes 1148936 | tf_op jit(solution)/shard_map/ppermute | solution.py:61
  69.6 19.7 %collective-permute-start.17 = (bf16[17,16,1088]{2,1,0:T(8,128)(2,1)S(1)}, bf16[17,16,1088]{2,1,0:T(8,128)(2,1)S(1)}, u32[]{:S(2)}, u32[]{:S(2)}) collective-permute-start(bf16[17,16,1088]{2,1,0:T(8,128)(2,1)S(1)} %bitcast.177), channel_id=1, source_target_pairs={{0,24},{4,28},{8,0},{12,4},{16,8},{20,12},{24,16},{28,20},{1,25},{... | collective-permute-start | bytes 1775624 | tf_op jit(solution)/shard_map/ppermute | solution.py:61
  70.8 18.6 %collective-permute-start.18 = (bf16[17,16,1088]{2,1,0:T(8,128)(2,1)S(1)}, bf16[17,16,1088]{2,1,0:T(8,128)(2,1)S(1)}, u32[]{:S(2)}, u32[]{:S(2)}) collective-permute-start(bf16[17,16,1088]{2,1,0:T(8,128)(2,1)S(1)} %collective-permute-done.15), channel_id=1, source_target_pairs={{0,4},{4,0},{8,12},{12,8},{16,20},{20,16},{24,28},{28,24},{1,5},{5... | collective-permute-start | bytes 1775624 | tf_op jit(solution)/shard_map/ppermute | solution.py:61
  72.2 17.1 %collective-permute-start.19 = (bf16[2,8,16,1088]{3,2,1,0:T(8,128)(2,1)S(1)}, bf16[2,8,16,1088]{3,2,1,0:T(8,128)(2,1)S(1)}, u32[]{:S(2)}, u32[]{:S(2)}) collective-permute-start(bf16[2,8,16,1088]{3,2,1,0:T(8,128)(2,1)S(1)} %bitcast.179), channel_id=1, source_target_pairs={{0,1},{1,0},{2,3},{3,2},{4,5},{5,4},{6,7},{7,6},{8,9},{9,8},{10,11... | collective-permute-start | bytes 1671176 | tf_op jit(solution)/shard_map/ppermute | solution.py:61
  72.2 17.1 %collective-permute-start.20 = (bf16[2,8,16,1088]{3,2,1,0:T(8,128)(2,1)S(1)}, bf16[2,8,16,1088]{3,2,1,0:T(8,128)(2,1)S(1)}, u32[]{:S(2)}, u32[]{:S(2)}) collective-permute-start(bf16[2,8,16,1088]{3,2,1,0:T(8,128)(2,1)S(1)} %collective-permute-done.11), channel_id=1, source_target_pairs={{0,1},{1,0},{2,3},{3,2},{4,5},{5,4},{6,7},{7,6},{8,9},{9,8},{10,11... | collective-permute-start | bytes 1671176 | tf_op jit(solution)/shard_map/ppermute | solution.py:61
  94.9 20.3 %collective-permute-start.24 = (bf16[17,16,1088]{2,1,0:T(8,128)(2,1)S(1)}, bf16[17,16,1088]{2,1,0:T(8,128)(2,1)S(1)}, u32[]{:S(2)}, u32[]{:S(2)}) collective-permute-start(bf16[17,16,1088]{2,1,0:T(8,128)(2,1)S(1)} %collective-permute-done.17), channel_id=1, source_target_pairs={{0,4},{4,0},{8,12},{12,8},{16,20},{20,16},{24,28},{28,24},{1,5},{5... | collective-permute-start | bytes 1775624 | tf_op jit(solution)/shard_map/ppermute | solution.py:61
  96.3 17.9 %collective-permute-start.22 = (bf16[2,8,16,1088]{3,2,1,0:T(8,128)(2,1)S(1)}, bf16[2,8,16,1088]{3,2,1,0:T(8,128)(2,1)S(1)}, u32[]{:S(2)}, u32[]{:S(2)}) collective-permute-start(bf16[2,8,16,1088]{3,2,1,0:T(8,128)(2,1)S(1)} %bitcast.227), channel_id=1, source_target_pairs={{0,2},{2,0},{1,3},{3,1},{4,6},{6,4},{5,7},{7,5},{8,10},{10,8},{9,1... | collective-permute-start | bytes 1671176 | tf_op jit(solution)/shard_map/ppermute | solution.py:61
  118.5 18.1 %collective-permute-start.26 = (bf16[2,8,16,1088]{3,2,1,0:T(8,128)(2,1)}, bf16[2,8,16,1088]{3,2,1,0:T(8,128)(2,1)S(1)}, u32[]{:S(2)}, u32[]{:S(2)}) collective-permute-start(bf16[2,8,16,1088]{3,2,1,0:T(8,128)(2,1)} %bitcast.214), channel_id=1, source_target_pairs={{0,2},{2,0},{1,3},{3,1},{4,6},{6,4},{5,7},{7,5},{8,10},{10,8},{9,1... | collective-permute-start | bytes 1671176 | tf_op jit(solution)/shard_map/ppermute | solution.py:61
  210.9 33.9 %collective-permute-start.42 = (bf16[10,16,1088]{2,1,0:T(8,128)(2,1)S(1)}, bf16[10,16,1088]{2,1,0:T(8,128)(2,1)S(1)}, u32[]{:S(2)}, u32[]{:S(2)}) collective-permute-start(bf16[10,16,1088]{2,1,0:T(8,128)(2,1)S(1)} %bitcast.240), channel_id=1, source_target_pairs={{16,0},{20,4},{24,8},{28,12},{0,16},{4,20},{8,24},{12,28},{17,1},{... | collective-permute-start | bytes 1044488 | tf_op jit(solution)/shard_map/ppermute | solution.py:61
  211.0 33.8 %collective-permute-start.43 = (bf16[17,16,1088]{2,1,0:T(8,128)(2,1)}, bf16[17,16,1088]{2,1,0:T(8,128)(2,1)S(1)}, u32[]{:S(2)}, u32[]{:S(2)}) collective-permute-start(bf16[17,16,1088]{2,1,0:T(8,128)(2,1)} %bitcast.100), channel_id=1, source_target_pairs={{24,0},{28,4},{0,8},{4,12},{8,16},{12,20},{16,24},{20,28},{25,1},{... | collective-permute-start | bytes 1775624 | tf_op jit(solution)/shard_map/ppermute | solution.py:61
  213.6 31.2 %collective-permute-start.44 = (bf16[17,16,1088]{2,1,0:T(8,128)(2,1)}, bf16[17,16,1088]{2,1,0:T(8,128)(2,1)S(1)}, u32[]{:S(2)}, u32[]{:S(2)}) collective-permute-start(bf16[17,16,1088]{2,1,0:T(8,128)(2,1)} %bitcast.102), channel_id=1, source_target_pairs={{0,4},{4,0},{8,12},{12,8},{16,20},{20,16},{24,28},{28,24},{1,5},{5... | collective-permute-start | bytes 1775624 | tf_op jit(solution)/shard_map/ppermute | solution.py:61
  214.5 30.4 %collective-permute-start.45 = (bf16[17,16,1088]{2,1,0:T(8,128)(2,1)}, bf16[17,16,1088]{2,1,0:T(8,128)(2,1)S(1)}, u32[]{:S(2)}, u32[]{:S(2)}) collective-permute-start(bf16[17,16,1088]{2,1,0:T(8,128)(2,1)} %bitcast.104), channel_id=1, source_target_pairs={{0,4},{4,0},{8,12},{12,8},{16,20},{20,16},{24,28},{28,24},{1,5},{5... | collective-permute-start | bytes 1775624 | tf_op jit(solution)/shard_map/ppermute | solution.py:61
  251.2 17.9 %collective-permute-start.47 = (bf16[2,8,16,1088]{3,2,1,0:T(8,128)(2,1)S(1)}, bf16[2,8,16,1088]{3,2,1,0:T(8,128)(2,1)S(1)}, u32[]{:S(2)}, u32[]{:S(2)}) collective-permute-start(bf16[2,8,16,1088]{3,2,1,0:T(8,128)(2,1)S(1)} %bitcast.226), channel_id=1, source_target_pairs={{0,2},{2,0},{1,3},{3,1},{4,6},{6,4},{5,7},{7,5},{8,10},{10,8},{9,1... | collective-permute-start | bytes 1671176 | tf_op jit(solution)/shard_map/ppermute | solution.py:61
  269.1 16.8 %collective-permute-start.51 = (bf16[10,16,1088]{2,1,0:T(8,128)(2,1)}, bf16[10,16,1088]{2,1,0:T(8,128)(2,1)}, u32[]{:S(2)}, u32[]{:S(2)}) collective-permute-start(bf16[10,16,1088]{2,1,0:T(8,128)(2,1)} %bitcast.116), channel_id=1, source_target_pairs={{8,0},{12,4},{16,8},{20,12},{24,16},{28,20},{0,24},{4,28},{9,1},{1... | collective-permute-start | bytes 1044488 | tf_op jit(solution)/shard_map/ppermute | solution.py:61
  272.2 23.6 %collective-permute-start.52 = (bf16[10,16,1088]{2,1,0:T(8,128)(2,1)}, bf16[10,16,1088]{2,1,0:T(8,128)(2,1)}, u32[]{:S(2)}, u32[]{:S(2)}) collective-permute-start(bf16[10,16,1088]{2,1,0:T(8,128)(2,1)} %bitcast.118), channel_id=1, source_target_pairs={{16,0},{20,4},{24,8},{28,12},{0,16},{4,20},{8,24},{12,28},{17,1},{... | collective-permute-start | bytes 1044488 | tf_op jit(solution)/shard_map/ppermute | solution.py:61
  273.0 22.8 %collective-permute-start.54 = (bf16[10,16,1088]{2,1,0:T(8,128)(2,1)}, bf16[10,16,1088]{2,1,0:T(8,128)(2,1)}, u32[]{:S(2)}, u32[]{:S(2)}) collective-permute-start(bf16[10,16,1088]{2,1,0:T(8,128)(2,1)} %bitcast.122), channel_id=1, source_target_pairs={{0,4},{4,0},{8,12},{12,8},{16,20},{20,16},{24,28},{28,24},{1,5},{5... | collective-permute-start | bytes 1044488 | tf_op jit(solution)/shard_map/ppermute | solution.py:61
  (103 other events, 1303.9 us)
where the time goes:
time: 328 us; the launch traced here: 324 us
  waiting for transfers between devices  120 us (37%)
  Pallas kernels  107 us (33%)
  starting transfers between devices  62.2 us (19%)
  other arithmetic  20.9 us (6%)
  local copies, waits for them, and re-layouts  12.2 us (4%)
    ppermute x54, waiting for transfers between devices, send(): return lax.ppermute(cut, axes, pairs).reshape(value.shape)  115 us
    ppermute x54, starting transfers between devices, send(): return lax.ppermute(cut, axes, pairs).reshape(value.shape)  51.9 us
    pallas_call x1, Pallas kernels, attend_pull(): pl.pallas_call(attend_pull_kernel, grid=(micro,), in_specs=[SCALARS] + [o...  29.2 us
    pallas_call x1, Pallas kernels, attend(): pl.pallas_call(attend_kernel, grid=(micro,), in_specs=[SCALARS] + [per((r...  15.8 us
    pallas_call x1, Pallas kernels, feed_forward(): pl.pallas_call(partial(feed_kernel, parts), grid=(micro,), in_specs=[per(...  14.4 us
    pallas_call x1, Pallas kernels, feed_grads(): pl.pallas_call(feed_grads_kernel, grid=(2,), in_specs=[whole(a) for a in...  12.3 us
    pallas_call x1, Pallas kernels, feed_out(): pl.pallas_call(partial(feed_out_kernel, parts), grid=(micro,), in_specs=[...  7.94 us
    unnamed x135, local copies, waits for them, and re-layouts  7.71 us
  transfers between devices with their start and end apart: 64, of which 24 were waited for; matrix products, arithmetic and copies ran while one was open for 6% of the time, Pallas kernels for 26%

commit v1 on v0

--- a/solution.py
+++ b/solution.py
@@ -207,7 +207,7 @@
     square = (128, row.shape[1])
     first_col = jnp.transpose(jnp.broadcast_to(first, square))[:, :1]
     own_col = jnp.transpose(jnp.broadcast_to(own, square))[:, :1]
-    allowed = (own <= own_col) & (first == first_col)
+    allowed = (own_col <= own) & (first_col == first)
     mask_ref[...] = jnp.where(allowed, 0.0, NEG_FILL)
 
 
@@ -253,13 +253,13 @@
         lanes = [slice(i * width + head * HEAD_DIM, i * width + (head + 1) * HEAD_DIM) for i in range(3)]
         queries, keys, values = [qkv_ref[0, :, part] for part in lanes]
         queries = queries * jnp.asarray(HEAD_DIM ** (-0.5), BF)
-        scores = dot(queries, keys, 1, 1) + mask_ref[...]
-        top = jnp.max(scores, axis=1, keepdims=True)
+        scores = dot(keys, queries, 1, 1) + mask_ref[...]
+        top = jnp.max(scores, axis=0, keepdims=True)
         weights = jnp.exp(scores - top)
-        total = jnp.sum(weights, axis=1, keepdims=True)
+        total = jnp.sum(weights, axis=0, keepdims=True)
         probs = (weights * (1.0 / total)).astype(BF)
-        log_ref[0, :, head : head + 1] = top + jnp.log(total)
-        heads_ref[0, :, lanes[0]] = dot(probs, values, 1, 0).astype(BF)
+        log_ref[0, head : head + 1, :] = top + jnp.log(total)
+        heads_ref[0, :, lanes[0]] = jnp.transpose(dot(values, probs, 0, 0)).astype(BF)
     branch = dot(heads_ref[0], weight_ref[3 * width :, :], 1, 0)
     write_halves(branch, rows, keep_ref, other_ref, send_ref)
 
@@ -275,13 +275,13 @@
         in_specs=[SCALARS] + [per((rows, model))] * 4
         + [whole(b) for b in near + side] + [per(row.shape[1:])],
         out_specs=[
-            per((group, model)), per((group, 3 * width)), per((group, 128)),
+            per((group, model)), per((group, 3 * width)), per((8, group)),
             per((group, width)), full((8, model)), full((24, model // 2)),
             per((rows, model)), per((rows, model)), per((2 * rows, model)),
         ],
         out_shape=[
             shape_of(BF, micro, group, model), shape_of(BF, micro, group, 3 * width),
-            shape_of(F32, micro, group, 128), shape_of(BF, micro, group, width),
+            shape_of(F32, micro, 8, group), shape_of(BF, micro, group, width),
             shape_of(F32, 8, model),
             shape_of(F32, 24, model // 2), shape_of(F32, micro, rows, model),
             shape_of(BF, micro, rows, model), shape_of(BF, micro, 2 * rows, model),
@@ -618,16 +618,15 @@
     for head in range(count):
         lanes = [slice(i * width + head * HEAD_DIM, i * width + (head + 1) * HEAD_DIM) for i in range(3)]
         queries, keys, values = [qkv_ref[0, :, part] for part in lanes]
-        scores = dot(queries * jnp.asarray(scale, BF), keys, 1, 1) + mask_ref[...]
-        probs = jnp.exp(scores - log_ref[0, :, head : head + 1])
+        scores = dot(keys, queries * jnp.asarray(scale, BF), 1, 1) + mask_ref[...]
+        probs = jnp.exp(scores - log_ref[0, head : head + 1, :])
         grad = grad_heads[:, lanes[0]]
-        delta = jnp.sum(
-            grad.astype(F32) * heads_ref[0, :, lanes[0]].astype(F32), axis=1, keepdims=True
-        )
-        grad_scores = (probs * (dot(grad, values, 1, 1) - delta)).astype(BF)
-        grad_qkv_ref[:, lanes[0]] = (scale * dot(grad_scores, keys, 1, 0)).astype(BF)
-        grad_qkv_ref[:, lanes[1]] = (scale * dot(grad_scores, queries, 0, 0)).astype(BF)
-        grad_qkv_ref[:, lanes[2]] = dot(probs.astype(BF), grad, 0, 0).astype(BF)
+        product = grad.astype(F32) * heads_ref[0, :, lanes[0]].astype(F32)
+        delta = jnp.sum(jnp.transpose(product), axis=0, keepdims=True)
+        grad_scores = (probs * (dot(values, grad, 1, 1) - delta)).astype(BF)
+        grad_qkv_ref[:, lanes[0]] = jnp.transpose(scale * dot(keys, grad_scores, 0, 0)).astype(BF)
+        grad_qkv_ref[:, lanes[1]] = (scale * dot(grad_scores, queries, 1, 0)).astype(BF)
+        grad_qkv_ref[:, lanes[2]] = dot(probs.astype(BF), grad, 1, 0).astype(BF)
     write_halves(dot(grad_qkv_ref[...], weight_ref[: 3 * width, :], 1, 0), rows, keep_ref, other_ref, send_ref)
     qkv_part = dot(grad_qkv_ref[...], normed_ref[0], 0, 0)
     out_part = dot(heads_ref[0], grad_ref[...], 0, 0)
@@ -679,7 +678,7 @@
         attend_pull_kernel,
         grid=(micro,),
         in_specs=[SCALARS] + [one] * 4 + [whole(b) for b in near + side] + [
-            per(row.shape[1:]), per((group, 3 * width)), per((group, 128)),
+            per(row.shape[1:]), per((group, 3 * width)), per((8, group)),
             per((group, width)), per((group, model)),
         ],
         out_specs=[one, one, per((2 * rows, model))] + [full(block)] * 8 + [full((2, model))],
@@ -818,12 +817,15 @@
     return lax.dynamic_slice_in_dim(wide, 8 * ctx, width, axis=0)
 
 
-def vector_sides(part, y, ctx):
+def vector_rows(part, ctx):
     table = part.reshape(8, 4, -1).transpose(1, 0, 2)
     mine = jnp.stack([pick(table, ctx ^ j) for j in (0, 1)])
     far = jnp.stack([pick(table, ctx ^ j) for j in (2, 3)])
     mine = mine + lax.ppermute(far, "ctx", CHIP_PAIRS)
-    mine = mine[0] + lax.ppermute(mine[1], "ctx", CORE_PAIRS)
+    return mine[0] + lax.ppermute(mine[1], "ctx", CORE_PAIRS)
+
+
+def vector_sides(mine, y):
     sides = mine.reshape(4, 2, -1).transpose(1, 0, 2)
     return pick(sides, y) + lax.ppermute(pick(sides, 1 - y), "dp", SIDE_PAIRS)
 
@@ -865,27 +867,30 @@
     n0, n1, n2, n3, s0, s1, s2, s3, t0, t1, t2, t3, g0, g1, b0, b1 = hold(
         [n0, n1, n2, n3, s0, s1, s2, s3, t0, t1, t2, t3, g0, g1, b0, b1]
     )
-    b3, b2, c1 = to_shift(b0, 3), to_shift(b0[: THIRDS[0]], 2), to_side(b1)
-    g2, g3 = to_core(g0), to_core(g1)
+    b3, b2, c1, d0 = (
+        to_shift(b0, 3), to_shift(b0[: THIRDS[0]], 2), to_side(b1), to_side(b0[CUT:])
+    )
     normed_one, qkv, log_total, heads, lines, rest, keep, other, away = attend(
         place, [t0, t1, t2, t3], [n0, n1, n3, n2], [s0, s1, s3, s2], row_info
     )
-    away, keep, other, b0, b1, b2, b3, c1, g0, g1, g2, g3 = hold(
-        [away, keep, other, b0, b1, b2, b3, c1, g0, g1, g2, g3]
+    away, keep, other, b0, b1, b2, b3, c1, d0, g0, g1 = hold(
+        [away, keep, other, b0, b1, b2, b3, c1, d0, g0, g1]
     )
     arrived = to_core(away)
-    away, arrived, keep, b0, b2, b3 = hold([half_sum(other, arrived), arrived, keep, b0, b2, b3])
-    across, d2, c3, c2 = (
-        to_chip(away), to_shift(b0[THIRDS[0] : THIRDS[1]], 2), to_side(b3), to_side(b2)
-    )
-    across, arrived, keep, b0, d2, c3, c2 = hold([across, arrived, keep, b0, d2, c3, c2])
+    away, arrived, keep, b0, b2, b3, g0, g1 = hold(
+        [half_sum(other, arrived), arrived, keep, b0, b2, b3, g0, g1]
+    )
+    across, d2, c3 = to_chip(away), to_shift(b0[THIRDS[0] : THIRDS[1]], 2), to_side(b3)
+    g2, g3 = to_core(g0), to_core(g1)
+    across, arrived, keep, b0, d2, c3, b2, g2, g3 = hold(
+        [across, arrived, keep, b0, d2, c3, b2, g2, g3]
+    )
     middle, h0 = middle_rows(tokens, keep, arrived, across, lines)
-    h0, middle, b0, d2 = hold([h0, middle, b0, d2])
-    h1, h2, e2, f2 = to_chip(h0), to_core(h0), to_shift(b0[THIRDS[1] :], 2), to_side(d2)
-    d0 = to_side(b0[CUT:])
+    h0, middle, b0, d2, b2 = hold([h0, middle, b0, d2, b2])
+    h1, e2, f2, c2 = to_chip(h0), to_shift(b0[THIRDS[1] :], 2), to_side(d2), to_side(b2)
     up_bias = own_up_bias(rest, order, width)
-    h0, h1, h2, e2, f2, d0, up_bias = hold([h0, h1, h2, e2, f2, d0, up_bias])
-    h3, a2 = to_core(h1), to_side(e2)
+    h0, h1, e2, f2, c2, up_bias = hold([h0, h1, e2, f2, c2, up_bias])
+    h2, h3, a2 = to_core(h0), to_core(h1), to_side(e2)
     blocks = [[c2, f2, a2], [b2, d2, e2], [b0], [c0, d0], [b1], [c1], [b3], [c3]]
     pull = feed_pull([g0, g1, g2, g3], blocks)
     h0, h1, h2, h3, pull = hold([h0, h1, h2, h3, pull], a2)
@@ -939,17 +944,19 @@
     k1, k2, k3, l0, part, feed_across, input_grad = hold(
         [k1, k2, both(k3, l3).astype(BF), l0, part, feed_across, input_grad]
     )
-    k3, part = to_shift(k3, 3, True), vector_sides(part, y, ctx)
+    k3, part = to_shift(k3, 3, True), vector_rows(part, ctx)
+    k1, k2, k3, part = hold([k1, k2, k3, part])
+    own = both(k0, l0) + k1.astype(F32) + k2.astype(F32) + k3.astype(F32)
+    attn_owned = aligned_owned(own, odd, ctx, width).T
+    part = vector_sides(part, y)
     mixed = mixed_rows(middle, feed_keep, feed_arrived, feed_across, lines)
     terms = [p0, q0, r1, jnp.concatenate([r2, t2], axis=0), r3]
     down_owned = sum(t[:width].astype(F32) for t in terms)
     up_owned = sum(t[width:].astype(F32) for t in terms).T
-    k3, part, mixed, down_owned, up_owned = hold([k3, part, mixed, down_owned, up_owned])
-    own = both(k0, l0) + k1.astype(F32) + k2.astype(F32) + k3.astype(F32)
-    attn_owned = aligned_owned(own, odd, ctx, width)
-    return (
-        mixed, input_grad, attn_owned.T, up_owned, down_owned, vector_owned(part, z),
-    )
+    part, mixed, down_owned, up_owned, attn_owned = hold(
+        [part, mixed, down_owned, up_owned, attn_owned]
+    )
+    return mixed, input_grad, attn_owned, up_owned, down_owned, vector_owned(part, z)
 
 
 def plain(tokens, cotangent, w_attn, w_up, w_down, vectors, segments):

time: 328 us -> 322 us (0.982)
  Pallas kernels: 107 us -> 103 us
    pallas_call x1, Pallas kernels: 29.2 us -> 24.9 us  [attend_pull(): pl.pallas_call(attend_pull_kernel, grid=(micro,), in_specs=[SCALARS] + [o...]
    unnamed x135 -> x137, local copies, waits for them, and re-layouts: 7.71 us -> 8.02 us
  transfers between devices with their start and end apart: 64 -> 64, of which waited for: 24 -> 28; matrix products, arithmetic and copies ran while one was open for 6% -> 6% of each run, Pallas kernels for 26% -> 25%
where the time goes in v1:
time: 322 us; the launch traced here: 319 us
  waiting for transfers between devices  120 us (37%)
  Pallas kernels  103 us (32%)
  starting transfers between devices  60.2 us (19%)
  other arithmetic  20.9 us (6%)
  local copies, waits for them, and re-layouts  12.6 us (4%)
    ppermute x54, waiting for transfers between devices, send(): return lax.ppermute(cut, axes, pairs).reshape(value.shape)  113 us
    ppermute x54, starting transfers between devices, send(): return lax.ppermute(cut, axes, pairs).reshape(value.shape)  50.2 us
    pallas_call x1, Pallas kernels, attend_pull(): pl.pallas_call(attend_pull_kernel, grid=(micro,), in_specs=[SCALARS] + [o...  24.9 us
    pallas_call x1, Pallas kernels, attend(): pl.pallas_call(attend_kernel, grid=(micro,), in_specs=[SCALARS] + [per((r...  16.4 us
    pallas_call x1, Pallas kernels, feed_forward(): pl.pallas_call(partial(feed_kernel, parts), grid=(micro,), in_specs=[per(...  14.4 us
    pallas_call x1, Pallas kernels, feed_grads(): pl.pallas_call(feed_grads_kernel, grid=(2,), in_specs=[whole(a) for a in...  12.3 us
    unnamed x137, local copies, waits for them, and re-layouts  8.02 us
    pallas_call x1, Pallas kernels, feed_pull(): pl.pallas_call(partial(pull_kernel, parts), grid=(micro,), in_specs=[per(...  7.71 us
  transfers between devices with their start and end apart: 64, of which 28 were waited for; matrix products, arithmetic and copies ran while one was open for 6% of the time, Pallas kernels for 25%

profile of v1, /device:TPU:0, one launch (start us, length us, event | category | flops | bytes accessed | tf_op | source)
XLA Modules:
  0.0 318.8 jit_solution(9552669158981902171)
XLA Ops:
  17.5 15.3 %collective-permute-done.7 = bf16[9,16,1088]{2,1,0:T(8,128)(2,1)} collective-permute-done((bf16[9,16,1088]{2,1,0:T(8,128)(2,1)S(1)}, bf16[9,16,1088]{2,1,0:T(8,128)(2,1)}, u32[]{:S(2)}, u32[]{:S(2)}) %collective-permute-start.7) | collective-permute-done | bytes 313376 | tf_op jit(solution)/shard_map/ppermute | solution.py:61
  36.2 16.7 %collective-permute-done.8 = bf16[11,16,1088]{2,1,0:T(8,128)(2,1)S(1)} collective-permute-done((bf16[11,16,1088]{2,1,0:T(8,128)(2,1)S(1)}, bf16[11,16,1088]{2,1,0:T(8,128)(2,1)S(1)}, u32[]{:S(2)}, u32[]{:S(2)}) %collective-permute-start.8) | collective-permute-done | bytes 383008 | tf_op jit(solution)/shard_map/ppermute | solution.py:61
  55.9 9.9 %collective-permute-done.12 = bf16[11,16,1088]{2,1,0:T(8,128)(2,1)S(1)} collective-permute-done((bf16[11,16,1088]{2,1,0:T(8,128)(2,1)S(1)}, bf16[11,16,1088]{2,1,0:T(8,128)(2,1)S(1)}, u32[]{:S(2)}, u32[]{:S(2)}) %collective-permute-start.12) | collective-permute-done | bytes 383008 | tf_op jit(solution)/shard_map/ppermute | solution.py:61
  65.8 3.9 %collective-permute-done.15 = bf16[17,16,1088]{2,1,0:T(8,128)(2,1)S(1)} collective-permute-done((bf16[17,16,1088]{2,1,0:T(8,128)(2,1)S(1)}, bf16[17,16,1088]{2,1,0:T(8,128)(2,1)S(1)}, u32[]{:S(2)}, u32[]{:S(2)}) %collective-permute-start.15) | collective-permute-done | bytes 591904 | tf_op jit(solution)/shard_map/ppermute | solution.py:61
  72.9 16.4 %attend.1 = (bf16[2,512,1088]{2,1,0:T(8,128)(2,1)}, bf16[2,512,960]{2,1,0:T(8,128)(2,1)}, f32[2,8,512]{2,1,0:T(8,128)}, bf16[2,512,320]{2,1,0:T(8,128)(2,1)}, f3...) custom-call(s32[3]{0:T(128)} %pad_add_fusion.3.place_ref, ...), custom_call_target="tpu_custom_call" | custom-call | flops 2852126720 | bytes 13369344 | tf_op jit(solution)/shard_map/attend/pallas_call | solution.py:272
  101.5 11.2 %collective-permute-done.22 = bf16[6,16,1088]{2,1,0:T(8,128)(2,1)S(1)} collective-permute-done((bf16[6,16,1088]{2,1,0:T(8,128)(2,1)S(1)}, bf16[6,16,1088]{2,1,0:T(8,128)(2,1)S(1)}, u32[]{:S(2)}, u32[]{:S(2)}) %collective-permute-start.22) | collective-permute-done | bytes 208928 | tf_op jit(solution)/shard_map/ppermute | solution.py:61
  114.7 3.3 %middle_rows.1 = (f32[2,128,1088]{2,1,0:T(8,128)}, bf16[2,128,1088]{2,1,0:T(8,128)(2,1)}) custom-call(bf16[2,128,1088]{2,1,0:T(8,128)(2,1)} %copy-done.2, f32[2,128,1088]{2,1,0:T(8,128)} %get-tuple-element.274.keep_ref, bf16[2,256,1088]{2,1,0:T(8,128)(2,1)} %bitcast.188, bf16[2,128,1088]{2,1,0:T(8,128)(2,1)} %bitcast.232, f32[8,1088]{1,0:T(8,128)} %get-tuple-element.277.vec_ref), custom_call_target="tpu_custom_call" | custom-call | tf_op jit(solution)/shard_map/middle_rows/pallas_call | solution.py:315
  125.3 6.1 %collective-permute-done.29 = bf16[4,16,1088]{2,1,0:T(8,128)(2,1)S(1)} collective-permute-done((bf16[4,16,1088]{2,1,0:T(8,128)(2,1)S(1)}, bf16[4,16,1088]{2,1,0:T(8,128)(2,1)S(1)}, u32[]{:S(2)}, u32[]{:S(2)}) %collective-permute-start.29) | collective-permute-done | bytes 139296 | tf_op jit(solution)/shard_map/ppermute | solution.py:61
  134.2 7.7 %feed_pull.1.pull_ref = bf16[2,512,1088]{2,1,0:T(8,128)(2,1)} custom-call(bf16[2,128,1088]{2,1,0:T(8,128)(2,1)} %copy-done.1, bf16[2,128,1088]{2,1,0:T(8,128)(2,1)} %bitcast.206, bf16[2,128,1088]{2,1,0:T(8,128)(2,1)} %bitcast.209, bf16[2,128,1088]{2,1,0:T(8,128)(2,1)} %bitcast.212, bf16[64,1088]{1,0:T(8,128)(2,1)} %bitcast.310, bf16[96,1088]{1,0:T(8,128)(2,1)} %bitcast.305, ...), custom_call_target="tpu_custom_call" | custom-call | flops 2424307712 | bytes 8912896 | tf_op jit(solution)/shard_map/feed_pull/pallas_call | solution.py:364
  143.3 14.4 %feed_forward.1 = (bf16[2,512,1088]{2,1,0:T(8,128)(2,1)}, bf16[2,512,1088]{2,1,0:T(8,128)(2,1)}, f32[2,128,1088]{2,1,0:T(8,128)}, bf16[2,128,1088]{2,1,0:T(8,128...) custom-call(bf16[2,128,1088]{2,1,0:T(8,128)(2,1)} %get-tuple-element.300.x0, bf16[2,128,1088]{2,1,0:T(8,128)(2,1)} %bitcast.217, ...), custom_call_target="tpu_custom_call" | custom-call | flops 4848615424 | bytes 13369344 | tf_op jit(solution)/shard_map/feed_forward/pallas_call | solution.py:415
  157.8 5.1 %feed_grads_first.1 = bf16[272,1088]{1,0:T(8,128)(2,1)} custom-call(bf16[1024,1088]{1,0:T(8,128)(2,1)} %bitcast.191, bf16[1024,1088]{1,0:T(8,128)(2,1)} %bitcast.193, bf16[2,128,1088]{2,1,0:T(8,128)(2,1)} %copy-done.1, bf16[2,128,1088]{2,1,0:T(8,128)(2,1)} %bitcast.207, bf16[2,128,1088]{2,1,0:T(8,128)(2,1)} %bitcast.210, bf16[2,128,1088]{2,1,0:T(8,128)(2,1)} %bitcast.213, ...), custom_call_target="tpu_custom_call" | custom-call | flops 606076928 | bytes 8912896 | tf_op jit(solution)/shard_map/feed_grads_first/pallas_call | solution.py:546
  167.0 12.3 %feed_grads.1 = (bf16[272,1088]{1,0:T(8,128)(2,1)}, bf16[272,1088]{1,0:T(8,128)(2,1)}, bf16[272,1088]{1,0:T(8,128)(2,1)}, bf16[272,1088]{1,0:T(8,128)(2,1)}, bf1...) custom-call(bf16[1024,1088]{1,0:T(8,128)(2,1)} %bitcast.192, ...), custom_call_target="tpu_custom_call" | custom-call | flops 4848615424 | bytes 13369344 | tf_op jit(solution)/shard_map/feed_grads/pallas_call | solution.py:500
  182.9 4.2 %middle_pull.1 = (f32[2,128,1088]{2,1,0:T(8,128)}, bf16[2,128,1088]{2,1,0:T(8,128)(2,1)}, f32[4,1088]{1,0:T(4,128)}) custom-call(bf16[2,128,1088]{2,1,0:T(8,128)(2,1)} %copy-done.1, f32[2,128,1088]{2,1,0:T(8,128)} %get-tuple-element.283.middle_ref, f32[2,128,1088]{2,1,0:T(8,128)} %get-tuple-element.318.keep_ref, bf16[2,256,1088]{2,1,0:T(8,128)(2,1)} %bitcast.190, ...), custom_call_target="tpu_custom_call" | custom-call | tf_op jit(solution)/shard_map/middle_pull/pallas_call | solution.py:584
  190.3 7.5 %feed_out.1 = (f32[2,128,1088]{2,1,0:T(8,128)}, bf16[2,128,1088]{2,1,0:T(8,128)(2,1)}, bf16[2,256,1088]{2,1,0:T(8,128)(2,1)}) custom-call(bf16[2,512,1088]{2,1,0:T(8,128)(2,1)} %get-tuple-element.329.active_ref, bf16[64,1088]{1,0:T(8,128)(2,1)} %bitcast.311, bf16[96,1088]{1,0:T(8,128)(2,1)} %bitcast.307, bf16[64,1088]{1,0:T(8,128)(2,1)} %bitcast.309, ...), custom_call_target="tpu_custom_call" | custom-call | flops 2424307712 | bytes 8912896 | tf_op jit(solution)/shard_map/feed_out/pallas_call | solution.py:450
  197.8 5.7 %collective-permute-done.38 = bf16[7,16,1088]{2,1,0:T(8,128)(2,1)S(1)} collective-permute-done((bf16[7,16,1088]{2,1,0:T(8,128)(2,1)S(1)}, bf16[7,16,1088]{2,1,0:T(8,128)(2,1)S(1)}, u32[]{:S(2)}, u32[]{:S(2)}) %collective-permute-start.38) | collective-permute-done | bytes 243744 | tf_op jit(solution)/shard_map/ppermute | solution.py:61
  208.4 3.2 %collective-permute-start.43 = (bf16[17,16,1088]{2,1,0:T(8,128)(2,1)}, bf16[17,16,1088]{2,1,0:T(8,128)(2,1)S(1)}, u32[]{:S(2)}, u32[]{:S(2)}) collective-permute-start(bf16[17,16,1088]{2,1,0:T(8,128)(2,1)} %bitcast.101), channel_id=1, source_target_pairs={{24,0},{28,4},{0,8},{4,12},{8,16},{12,20},{16,24},{20,28},{25,1},{... | collective-permute-start | bytes 1775624 | tf_op jit(solution)/shard_map/ppermute | solution.py:61
  213.7 24.9 %attend_pull.1 = (f32[2,128,1088]{2,1,0:T(8,128)}, bf16[2,128,1088]{2,1,0:T(8,128)(2,1)}, bf16[2,256,1088]{2,1,0:T(8,128)(2,1)}, bf16[160,1088]{1,0:T(8,128)(2,1...) custom-call(s32[3]{0:T(128)} %pad_add_fusion.3.place_ref, ...), custom_call_target="tpu_custom_call" | custom-call | flops 7130316800 | bytes 13369344 | tf_op jit(solution)/shard_map/attend_pull/pallas_call | solution.py:677
  250.7 6.5 %collective-permute-done.49 = bf16[10,16,1088]{2,1,0:T(8,128)(2,1)S(1)} collective-permute-done((bf16[10,16,1088]{2,1,0:T(8,128)(2,1)S(1)}, bf16[10,16,1088]{2,1,0:T(8,128)(2,1)S(1)}, u32[]{:S(2)}, u32[]{:S(2)}) %collective-permute-start.49) | collective-permute-done | bytes 348192 | tf_op jit(solution)/shard_map/ppermute | solution.py:61
  258.1 6.6 %collective-permute-done.50 = bf16[10,16,1088]{2,1,0:T(8,128)(2,1)S(1)} collective-permute-done((bf16[10,16,1088]{2,1,0:T(8,128)(2,1)S(1)}, bf16[10,16,1088]{2,1,0:T(8,128)(2,1)S(1)}, u32[]{:S(2)}, u32[]{:S(2)}) %collective-permute-start.50) | collective-permute-done | bytes 348192 | tf_op jit(solution)/shard_map/ppermute | solution.py:61
  269.7 4.1 %input_pull.1 = (bf16[2,1088,128]{2,1,0:T(8,128)(2,1)}, f32[2,1088]{1,0:T(2,128)}) custom-call(bf16[2,128,1088]{2,1,0:T(8,128)(2,1)} %copy-done.2, f32[2,128,1088]{2,1,0:T(8,128)} %get-tuple-element.388.grad_ref, f32[2,128,1088]{2,1,0:T(8,128)} %get-tuple-element.389.keep_ref, bf16[2,256,1088]{2,1,0:T(8,128)(2,1)} %bitcast.186, ...), custom_call_target="tpu_custom_call" | custom-call | tf_op jit(solution)/shard_map/input_pull/pallas_call | solution.py:724
  276.1 3.3 %collective-permute-done.53 = bf16[10,16,1088]{2,1,0:T(8,128)(2,1)} collective-permute-done((bf16[10,16,1088]{2,1,0:T(8,128)(2,1)}, bf16[10,16,1088]{2,1,0:T(8,128)(2,1)}, u32[]{:S(2)}, u32[]{:S(2)}) %collective-permute-start.53) | collective-permute-done | bytes 348192 | tf_op jit(solution)/shard_map/ppermute | solution.py:61
  281.4 9.7 %collective-permute-done.52 = bf16[10,16,1088]{2,1,0:T(8,128)(2,1)} collective-permute-done((bf16[10,16,1088]{2,1,0:T(8,128)(2,1)}, bf16[10,16,1088]{2,1,0:T(8,128)(2,1)}, u32[]{:S(2)}, u32[]{:S(2)}) %collective-permute-start.52) | collective-permute-done | bytes 348192 | tf_op jit(solution)/shard_map/ppermute | solution.py:61
  298.6 3.1 mixed_rows.1
  301.7 3.8 %collective-permute-done.56 = bf16[10,16,1088]{2,1,0:T(8,128)(2,1)S(1)} collective-permute-done((bf16[10,16,1088]{2,1,0:T(8,128)(2,1)}, bf16[10,16,1088]{2,1,0:T(8,128)(2,1)S(1)}, u32[]{:S(2)}, u32[]{:S(2)}) %collective-permute-start.56) | collective-permute-done | bytes 348192 | tf_op jit(solution)/shard_map/ppermute | solution.py:61
  (324 shorter events, 112.3 us)
Async XLA Ops:
  9.3 23.5 %collective-permute-start.6 = (bf16[2,8,16,1088]{3,2,1,0:T(8,128)(2,1)S(1)}, bf16[2,8,16,1088]{3,2,1,0:T(8,128)(2,1)}, u32[]{:S(2)}, u32[]{:S(2)}) collective-permute-start(bf16[2,8,16,1088]{3,2,1,0:T(8,128)(2,1)S(1)} %bitcast.181), channel_id=1, source_target_pairs={{0,2},{2,0},{1,3},{3,1},{4,6},{6,4},{5,7},{7,5},{8,10},{10,8},{9,1... | collective-permute-start | bytes 1671176 | tf_op jit(solution)/shard_map/ppermute | solution.py:61
  11.3 21.6 %collective-permute-start.3 = (bf16[11,16,1088]{2,1,0:T(8,128)(2,1)S(1)}, bf16[11,16,1088]{2,1,0:T(8,128)(2,1)S(1)}, u32[]{:S(2)}, u32[]{:S(2)}) collective-permute-start(bf16[11,16,1088]{2,1,0:T(8,128)(2,1)S(1)} %bitcast.235), channel_id=1, source_target_pairs={{0,8},{4,12},{8,16},{12,20},{16,24},{20,28},{24,0},{28,4},{1,9},{5... | collective-permute-start | bytes 1148936 | tf_op jit(solution)/shard_map/ppermute | solution.py:61
  12.9 20.0 %collective-permute-start.4 = (bf16[11,16,1088]{2,1,0:T(8,128)(2,1)S(1)}, bf16[11,16,1088]{2,1,0:T(8,128)(2,1)}, u32[]{:S(2)}, u32[]{:S(2)}) collective-permute-start(bf16[11,16,1088]{2,1,0:T(8,128)(2,1)S(1)} %bitcast.236), channel_id=1, source_target_pairs={{0,24},{4,28},{8,0},{12,4},{16,8},{20,12},{24,16},{28,20},{1,25},{... | collective-permute-start | bytes 1148936 | tf_op jit(solution)/shard_map/ppermute | solution.py:61
  15.1 17.8 %collective-permute-start.5 = (bf16[11,16,1088]{2,1,0:T(8,128)(2,1)S(1)}, bf16[11,16,1088]{2,1,0:T(8,128)(2,1)}, u32[]{:S(2)}, u32[]{:S(2)}) collective-permute-start(bf16[11,16,1088]{2,1,0:T(8,128)(2,1)S(1)} %bitcast.237), channel_id=1, source_target_pairs={{0,4},{4,0},{8,12},{12,8},{16,20},{20,16},{24,28},{28,24},{1,5},{5... | collective-permute-start | bytes 1148936 | tf_op jit(solution)/shard_map/ppermute | solution.py:61
  15.7 17.1 %collective-permute-start.7 = (bf16[9,16,1088]{2,1,0:T(8,128)(2,1)S(1)}, bf16[9,16,1088]{2,1,0:T(8,128)(2,1)}, u32[]{:S(2)}, u32[]{:S(2)}) collective-permute-start(bf16[9,16,1088]{2,1,0:T(8,128)(2,1)S(1)} %bitcast.242), channel_id=1, source_target_pairs={{0,4},{4,0},{8,12},{12,8},{16,20},{20,16},{24,28},{28,24},{1,5},{5... | collective-permute-start | bytes 940040 | tf_op jit(solution)/shard_map/ppermute | solution.py:61
  32.9 20.1 %collective-permute-start.11 = (bf16[2,8,16,1088]{3,2,1,0:T(8,128)(2,1)S(1)}, bf16[2,8,16,1088]{3,2,1,0:T(8,128)(2,1)S(1)}, u32[]{:S(2)}, u32[]{:S(2)}) collective-permute-start(bf16[2,8,16,1088]{3,2,1,0:T(8,128)(2,1)S(1)} %bitcast.179), channel_id=1, source_target_pairs={{0,2},{2,0},{1,3},{3,1},{4,6},{6,4},{5,7},{7,5},{8,10},{10,8},{9,1... | collective-permute-start | bytes 1671176 | tf_op jit(solution)/shard_map/ppermute | solution.py:61
  33.5 19.4 %collective-permute-start.8 = (bf16[11,16,1088]{2,1,0:T(8,128)(2,1)S(1)}, bf16[11,16,1088]{2,1,0:T(8,128)(2,1)S(1)}, u32[]{:S(2)}, u32[]{:S(2)}) collective-permute-start(bf16[11,16,1088]{2,1,0:T(8,128)(2,1)S(1)} %bitcast.238), channel_id=1, source_target_pairs={{0,16},{4,20},{8,24},{12,28},{16,0},{20,4},{24,8},{28,12},{1,17},{... | collective-permute-start | bytes 1148936 | tf_op jit(solution)/shard_map/ppermute | solution.py:61
  34.2 18.7 %collective-permute-start.9 = (bf16[11,16,1088]{2,1,0:T(8,128)(2,1)S(1)}, bf16[11,16,1088]{2,1,0:T(8,128)(2,1)S(1)}, u32[]{:S(2)}, u32[]{:S(2)}) collective-permute-start(bf16[11,16,1088]{2,1,0:T(8,128)(2,1)S(1)} %collective-permute-done.3), channel_id=1, source_target_pairs={{0,4},{4,0},{8,12},{12,8},{16,20},{20,16},{24,28},{28,24},{1,5},{5... | collective-permute-start | bytes 1148936 | tf_op jit(solution)/shard_map/ppermute | solution.py:61
  35.6 17.3 %collective-permute-start.10 = (bf16[11,16,1088]{2,1,0:T(8,128)(2,1)}, bf16[11,16,1088]{2,1,0:T(8,128)(2,1)S(1)}, u32[]{:S(2)}, u32[]{:S(2)}) collective-permute-start(bf16[11,16,1088]{2,1,0:T(8,128)(2,1)} %bitcast.25), channel_id=1, source_target_pairs={{0,4},{4,0},{8,12},{12,8},{16,20},{20,16},{24,28},{28,24},{1,5},{5... | collective-permute-start | bytes 1148936 | tf_op jit(solution)/shard_map/ppermute | solution.py:61
  53.0 16.7 %collective-permute-start.15 = (bf16[17,16,1088]{2,1,0:T(8,128)(2,1)S(1)}, bf16[17,16,1088]{2,1,0:T(8,128)(2,1)S(1)}, u32[]{:S(2)}, u32[]{:S(2)}) collective-permute-start(bf16[17,16,1088]{2,1,0:T(8,128)(2,1)S(1)} %bitcast.177), channel_id=1, source_target_pairs={{0,8},{4,12},{8,16},{12,20},{16,24},{20,28},{24,0},{28,4},{1,9},{5... | collective-permute-start | bytes 1775624 | tf_op jit(solution)/shard_map/ppermute | solution.py:61
  69.6 21.1 %collective-permute-start.17 = (bf16[17,16,1088]{2,1,0:T(8,128)(2,1)S(1)}, bf16[17,16,1088]{2,1,0:T(8,128)(2,1)S(1)}, u32[]{:S(2)}, u32[]{:S(2)}) collective-permute-start(bf16[17,16,1088]{2,1,0:T(8,128)(2,1)S(1)} %bitcast.178), channel_id=1, source_target_pairs={{0,24},{4,28},{8,0},{12,4},{16,8},{20,12},{24,16},{28,20},{1,25},{... | collective-permute-start | bytes 1775624 | tf_op jit(solution)/shard_map/ppermute | solution.py:61
  70.6 20.2 %collective-permute-start.18 = (bf16[17,16,1088]{2,1,0:T(8,128)(2,1)S(1)}, bf16[17,16,1088]{2,1,0:T(8,128)(2,1)S(1)}, u32[]{:S(2)}, u32[]{:S(2)}) collective-permute-start(bf16[17,16,1088]{2,1,0:T(8,128)(2,1)S(1)} %collective-permute-done.15), channel_id=1, source_target_pairs={{0,4},{4,0},{8,12},{12,8},{16,20},{20,16},{24,28},{28,24},{1,5},{5... | collective-permute-start | bytes 1775624 | tf_op jit(solution)/shard_map/ppermute | solution.py:61
  72.2 18.5 %collective-permute-start.19 = (bf16[8,16,1088]{2,1,0:T(8,128)(2,1)S(1)}, bf16[8,16,1088]{2,1,0:T(8,128)(2,1)S(1)}, u32[]{:S(2)}, u32[]{:S(2)}) collective-permute-start(bf16[8,16,1088]{2,1,0:T(8,128)(2,1)S(1)} %bitcast.244), channel_id=1, source_target_pairs={{0,4},{4,0},{8,12},{12,8},{16,20},{20,16},{24,28},{28,24},{1,5},{5... | collective-permute-start | bytes 835592 | tf_op jit(solution)/shard_map/ppermute | solution.py:61
  72.8 16.6 %collective-permute-start.16 = (bf16[4,16,1088]{2,1,0:T(8,128)(2,1)S(1)}, bf16[4,16,1088]{2,1,0:T(8,128)(2,1)S(1)}, u32[]{:S(2)}, u32[]{:S(2)}) collective-permute-start(bf16[4,16,1088]{2,1,0:T(8,128)(2,1)S(1)} %bitcast.249), channel_id=1, source_target_pairs={{0,16},{4,20},{8,24},{12,28},{16,0},{20,4},{24,8},{28,12},{1,17},{... | collective-permute-start | bytes 417800 | tf_op jit(solution)/shard_map/ppermute | solution.py:61
  95.6 18.3 %collective-permute-start.23 = (bf16[17,16,1088]{2,1,0:T(8,128)(2,1)S(1)}, bf16[17,16,1088]{2,1,0:T(8,128)(2,1)S(1)}, u32[]{:S(2)}, u32[]{:S(2)}) collective-permute-start(bf16[17,16,1088]{2,1,0:T(8,128)(2,1)S(1)} %collective-permute-done.17), channel_id=1, source_target_pairs={{0,4},{4,0},{8,12},{12,8},{16,20},{20,16},{24,28},{28,24},{1,5},{5... | collective-permute-start | bytes 1775624 | tf_op jit(solution)/shard_map/ppermute | solution.py:61
  164.3 17.1 %collective-permute-start.35 = (bf16[17,16,1088]{2,1,0:T(8,128)(2,1)S(1)}, bf16[17,16,1088]{2,1,0:T(8,128)(2,1)S(1)}, u32[]{:S(2)}, u32[]{:S(2)}) collective-permute-start(bf16[17,16,1088]{2,1,0:T(8,128)(2,1)S(1)} %bitcast.205), channel_id=1, source_target_pairs={{0,4},{4,0},{8,12},{12,8},{16,20},{20,16},{24,28},{28,24},{1,5},{5... | collective-permute-start | bytes 1775624 | tf_op jit(solution)/shard_map/ppermute | solution.py:61
  208.4 32.9 %collective-permute-start.42 = (bf16[10,16,1088]{2,1,0:T(8,128)(2,1)S(1)}, bf16[10,16,1088]{2,1,0:T(8,128)(2,1)S(1)}, u32[]{:S(2)}, u32[]{:S(2)}) collective-permute-start(bf16[10,16,1088]{2,1,0:T(8,128)(2,1)S(1)} %bitcast.241), channel_id=1, source_target_pairs={{16,0},{20,4},{24,8},{28,12},{0,16},{4,20},{8,24},{12,28},{17,1},{... | collective-permute-start | bytes 1044488 | tf_op jit(solution)/shard_map/ppermute | solution.py:61
  208.4 32.8 %collective-permute-start.43 = (bf16[17,16,1088]{2,1,0:T(8,128)(2,1)}, bf16[17,16,1088]{2,1,0:T(8,128)(2,1)S(1)}, u32[]{:S(2)}, u32[]{:S(2)}) collective-permute-start(bf16[17,16,1088]{2,1,0:T(8,128)(2,1)} %bitcast.101), channel_id=1, source_target_pairs={{24,0},{28,4},{0,8},{4,12},{8,16},{12,20},{16,24},{20,28},{25,1},{... | collective-permute-start | bytes 1775624 | tf_op jit(solution)/shard_map/ppermute | solution.py:61
  211.6 29.7 %collective-permute-start.44 = (bf16[17,16,1088]{2,1,0:T(8,128)(2,1)}, bf16[17,16,1088]{2,1,0:T(8,128)(2,1)S(1)}, u32[]{:S(2)}, u32[]{:S(2)}) collective-permute-start(bf16[17,16,1088]{2,1,0:T(8,128)(2,1)} %bitcast.103), channel_id=1, source_target_pairs={{0,4},{4,0},{8,12},{12,8},{16,20},{20,16},{24,28},{28,24},{1,5},{5... | collective-permute-start | bytes 1775624 | tf_op jit(solution)/shard_map/ppermute | solution.py:61
  212.8 28.5 %collective-permute-start.45 = (bf16[17,16,1088]{2,1,0:T(8,128)(2,1)}, bf16[17,16,1088]{2,1,0:T(8,128)(2,1)S(1)}, u32[]{:S(2)}, u32[]{:S(2)}) collective-permute-start(bf16[17,16,1088]{2,1,0:T(8,128)(2,1)} %bitcast.105), channel_id=1, source_target_pairs={{0,4},{4,0},{8,12},{12,8},{16,20},{20,16},{24,28},{28,24},{1,5},{5... | collective-permute-start | bytes 1775624 | tf_op jit(solution)/shard_map/ppermute | solution.py:61
  248.0 17.6 %collective-permute-start.47 = (bf16[2,8,16,1088]{3,2,1,0:T(8,128)(2,1)S(1)}, bf16[2,8,16,1088]{3,2,1,0:T(8,128)(2,1)S(1)}, u32[]{:S(2)}, u32[]{:S(2)}) collective-permute-start(bf16[2,8,16,1088]{3,2,1,0:T(8,128)(2,1)S(1)} %bitcast.227), channel_id=1, source_target_pairs={{0,2},{2,0},{1,3},{3,1},{4,6},{6,4},{5,7},{7,5},{8,10},{10,8},{9,1... | collective-permute-start | bytes 1671176 | tf_op jit(solution)/shard_map/ppermute | solution.py:61
  248.4 17.2 %collective-permute-start.48 = (bf16[17,16,1088]{2,1,0:T(8,128)(2,1)S(1)}, bf16[17,16,1088]{2,1,0:T(8,128)(2,1)S(1)}, u32[]{:S(2)}, u32[]{:S(2)}) collective-permute-start(bf16[17,16,1088]{2,1,0:T(8,128)(2,1)S(1)} %bitcast.203), channel_id=1, source_target_pairs={{8,0},{12,4},{16,8},{20,12},{24,16},{28,20},{0,24},{4,28},{9,1},{1... | collective-permute-start | bytes 1775624 | tf_op jit(solution)/shard_map/ppermute | solution.py:61
  267.6 23.4 %collective-permute-start.52 = (bf16[10,16,1088]{2,1,0:T(8,128)(2,1)}, bf16[10,16,1088]{2,1,0:T(8,128)(2,1)}, u32[]{:S(2)}, u32[]{:S(2)}) collective-permute-start(bf16[10,16,1088]{2,1,0:T(8,128)(2,1)} %bitcast.119), channel_id=1, source_target_pairs={{16,0},{20,4},{24,8},{28,12},{0,16},{4,20},{8,24},{12,28},{17,1},{... | collective-permute-start | bytes 1044488 | tf_op jit(solution)/shard_map/ppermute | solution.py:61
  268.5 22.6 %collective-permute-start.54 = (bf16[10,16,1088]{2,1,0:T(8,128)(2,1)}, bf16[10,16,1088]{2,1,0:T(8,128)(2,1)}, u32[]{:S(2)}, u32[]{:S(2)}) collective-permute-start(bf16[10,16,1088]{2,1,0:T(8,128)(2,1)} %bitcast.123), channel_id=1, source_target_pairs={{0,4},{4,0},{8,12},{12,8},{16,20},{20,16},{24,28},{28,24},{1,5},{5... | collective-permute-start | bytes 1044488 | tf_op jit(solution)/shard_map/ppermute | solution.py:61
  (104 other events, 1294.4 us)

commit v2 on v1

--- a/solution.py
+++ b/solution.py
@@ -513,9 +513,11 @@
 
 
 def feed_grads_first_kernel(
-    active_ref, grad_hidden_ref, g0, g1, g2, g3, x0, x1, x2, x3, out_ref, total_ref, right_ref
+    active_ref, grad_hidden_ref, g0, g1, g2, g3, x0, x1, x2, x3, first_ref, second_ref,
+    total_ref, right_ref,
 ):
-    each = out_ref.shape[0] // 2
+    each = total_ref.shape[0] // 2
+    cut = first_ref.shape[0]
     step = pl.program_id(0)
     for left_ref, refs, part in (
         (active_ref, (g0, g1, g2, g3), 0), (grad_hidden_ref, (x0, x1, x2, x3), 1)
@@ -534,7 +536,8 @@
 
     @pl.when(step == pl.num_programs(0) - 1)
     def _():
-        out_ref[...] = total_ref[...].astype(BF)
+        first_ref[...] = total_ref[:cut, :].astype(BF)
+        second_ref[...] = total_ref[cut:, :].astype(BF)
 
 
 def feed_grads_first(active, grad_hidden, grad, x):
@@ -547,8 +550,8 @@
         feed_grads_first_kernel,
         grid=(micro,),
         in_specs=[left] * 2 + [per((own, model))] * 8,
-        out_specs=full(block),
-        out_shape=shape_of(BF, *block),
+        out_specs=[full((BACK_CUT, model)), full((block[0] - BACK_CUT, model))],
+        out_shape=[shape_of(BF, BACK_CUT, model), shape_of(BF, block[0] - BACK_CUT, model)],
         scratch_shapes=[pltpu.VMEM(block, F32), pltpu.VMEM((group, model), BF)],
         compiler_params=params(56),
         cost_estimate=pl.CostEstimate(
@@ -900,23 +903,26 @@
     x_all, grad_all = [h0, h1, h2, h3], [g0, g1, g2, g3]
 
     arrived = to_core(away)
-    q2 = feed_grads_first(flat(active), flat(grad_hidden), grad_all, x_all)
-    away, arrived, keep, active, q2 = hold(
-        [half_sum(other, arrived), arrived, keep, active, q2]
-    )
-    across, q2 = to_chip(away), to_side(q2)
+    q2, v2 = feed_grads_first(flat(active), flat(grad_hidden), grad_all, x_all)
+    away, arrived, keep, active, q2, v2 = hold(
+        [half_sum(other, arrived), arrived, keep, active, q2, v2]
+    )
+    across, q2, v2 = to_chip(away), to_side(q2), to_side(v2)
     p2, p0, q0, p1, q1, p3, q3 = feed_grads(flat(active), flat(grad_hidden), grad_all, x_all)
-    across, arrived, keep, p2, q2 = hold([across, arrived, keep, p2, q2])
+    across, arrived, keep, p2, q2, v2 = hold([across, arrived, keep, p2, q2, v2])
     grad_middle, h0, sums = middle_pull(cotangent, middle, keep, arrived, across, lines)
-    h0, p2, q3, grad_middle, active = hold([h0, both(p2, q2).astype(BF), q3, grad_middle, active])
-    h1, h2, r2, q3 = to_chip(h0), to_core(h0), to_shift(p2[:BACK_CUT], 2, True), to_side(q3)
+    h0, q2, p2, v2, q3, grad_middle, active = hold(
+        [h0, both(p2[:BACK_CUT], q2).astype(BF), p2, v2, q3, grad_middle, active]
+    )
+    h1, h2, r2, q3 = to_chip(h0), to_core(h0), to_shift(q2, 2, True), to_side(q3)
+    p2 = both(p2[BACK_CUT:], v2).astype(BF)
     feed_keep, feed_other, feed_away = feed_out(active, blocks)
     h0, h1, h2, r2, q3, p2, feed_away = hold([h0, h1, h2, r2, q3, p2, feed_away])
     h3, feed_arrived = to_core(h1), to_core(feed_away)
     h0, h1, h2, h3, p2, p3, q1, q0, feed_arrived = hold(
         [h0, h1, h2, h3, p2, both(p3, q3).astype(BF), q1, q0, feed_arrived]
     )
-    t2, r3 = to_shift(p2[BACK_CUT:], 2, True), to_shift(p3, 3, True)
+    t2, r3 = to_shift(p2, 2, True), to_shift(p3, 3, True)
     q1, q0 = to_side(q1), to_side(q0)
     keep, other, away, *parts, bias_sums = attend_pull(
         place, [h0, h1, h2, h3], [n0, n1, n3, n2], [s0, s1, s3, s2], row_info,
@@ -953,9 +959,7 @@
     terms = [p0, q0, r1, jnp.concatenate([r2, t2], axis=0), r3]
     down_owned = sum(t[:width].astype(F32) for t in terms)
     up_owned = sum(t[width:].astype(F32) for t in terms).T
-    part, mixed, down_owned, up_owned, attn_owned = hold(
-        [part, mixed, down_owned, up_owned, attn_owned]
-    )
+    part, mixed, down_owned, up_owned = hold([part, mixed, down_owned, up_owned])
     return mixed, input_grad, attn_owned, up_owned, down_owned, vector_owned(part, z)
 
 
@@ -1005,7 +1009,7 @@
     mixed = mixed_rows(middle, *row_scatter(*feed_out(active, blocks)), lines)
     grad_middle, branch, sums = middle_pull(cotangent, middle, *row_scatter(*halves), lines)
     arrays = flat(active), flat(grad_hidden), grad_all, x_all
-    parts = [feed_grads_first(*arrays)] + list(feed_grads(*arrays))
+    parts = [jnp.concatenate(feed_grads_first(*arrays), axis=0)] + list(feed_grads(*arrays))
     down_owned, up_owned = [
         lax.psum_scatter(
             jnp.concatenate([p[i * each : (i + 1) * each] for p in parts], axis=0),

time: 322 us -> 322 us (level)
  starting transfers between devices: 60.2 us -> 63.7 us
    ppermute x54 -> x55, starting transfers between devices: 50.2 us -> 53.6 us  [send(): return lax.ppermute(cut, axes, pairs).reshape(value.shape)]
    unnamed x137 -> x141, local copies, waits for them, and re-layouts: 8.02 us -> 6.22 us
    ppermute x54 -> x55, waiting for transfers between devices: 113 us -> 114 us  [send(): return lax.ppermute(cut, axes, pairs).reshape(value.shape)]
  transfers between devices with their start and end apart: 64 -> 65, of which waited for: 28 -> 29; matrix products, arithmetic and copies ran while one was open for 6% -> 6% of each run, Pallas kernels for 25% -> 25%
where the time goes in v2:
time: 322 us; the launch traced here: 318 us
  waiting for transfers between devices  118 us (37%)
  Pallas kernels  103 us (32%)
  starting transfers between devices  63.7 us (20%)
  other arithmetic  20.7 us (6%)
  local copies, waits for them, and re-layouts  10.7 us (3%)
    ppermute x55, waiting for transfers between devices, send(): return lax.ppermute(cut, axes, pairs).reshape(value.shape)  114 us
    ppermute x55, starting transfers between devices, send(): return lax.ppermute(cut, axes, pairs).reshape(value.shape)  53.6 us
    pallas_call x1, Pallas kernels, attend_pull(): pl.pallas_call(attend_pull_kernel, grid=(micro,), in_specs=[SCALARS] + [o...  24.5 us
    pallas_call x1, Pallas kernels, attend(): pl.pallas_call(attend_kernel, grid=(micro,), in_specs=[SCALARS] + [per((r...  16.5 us
    pallas_call x1, Pallas kernels, feed_forward(): pl.pallas_call(partial(feed_kernel, parts), grid=(micro,), in_specs=[per(...  14.6 us
    pallas_call x1, Pallas kernels, feed_grads(): pl.pallas_call(feed_grads_kernel, grid=(2,), in_specs=[whole(a) for a in...  12.3 us
    pallas_call x1, Pallas kernels, feed_pull(): pl.pallas_call(partial(pull_kernel, parts), grid=(micro,), in_specs=[per(...  7.66 us
    pallas_call x1, Pallas kernels, feed_out(): pl.pallas_call(partial(feed_out_kernel, parts), grid=(micro,), in_specs=[...  7.55 us
  transfers between devices with their start and end apart: 65, of which 29 were waited for; matrix products, arithmetic and copies ran while one was open for 6% of the time, Pallas kernels for 25%

profile of v2, /device:TPU:0, one launch (start us, length us, event | category | flops | bytes accessed | tf_op | source)
XLA Modules:
  0.0 317.6 jit_solution(5784704284917420429)
XLA Ops:
  17.4 15.3 %collective-permute-done.7 = bf16[9,16,1088]{2,1,0:T(8,128)(2,1)} collective-permute-done((bf16[9,16,1088]{2,1,0:T(8,128)(2,1)S(1)}, bf16[9,16,1088]{2,1,0:T(8,128)(2,1)}, u32[]{:S(2)}, u32[]{:S(2)}) %collective-permute-start.7) | collective-permute-done | bytes 313376 | tf_op jit(solution)/shard_map/ppermute | solution.py:61
  36.1 16.7 %collective-permute-done.8 = bf16[11,16,1088]{2,1,0:T(8,128)(2,1)S(1)} collective-permute-done((bf16[11,16,1088]{2,1,0:T(8,128)(2,1)S(1)}, bf16[11,16,1088]{2,1,0:T(8,128)(2,1)S(1)}, u32[]{:S(2)}, u32[]{:S(2)}) %collective-permute-start.8) | collective-permute-done | bytes 383008 | tf_op jit(solution)/shard_map/ppermute | solution.py:61
  55.8 9.9 %collective-permute-done.12 = bf16[11,16,1088]{2,1,0:T(8,128)(2,1)S(1)} collective-permute-done((bf16[11,16,1088]{2,1,0:T(8,128)(2,1)S(1)}, bf16[11,16,1088]{2,1,0:T(8,128)(2,1)S(1)}, u32[]{:S(2)}, u32[]{:S(2)}) %collective-permute-start.12) | collective-permute-done | bytes 383008 | tf_op jit(solution)/shard_map/ppermute | solution.py:61
  65.6 3.9 %collective-permute-done.15 = bf16[17,16,1088]{2,1,0:T(8,128)(2,1)S(1)} collective-permute-done((bf16[17,16,1088]{2,1,0:T(8,128)(2,1)S(1)}, bf16[17,16,1088]{2,1,0:T(8,128)(2,1)S(1)}, u32[]{:S(2)}, u32[]{:S(2)}) %collective-permute-start.15) | collective-permute-done | bytes 591904 | tf_op jit(solution)/shard_map/ppermute | solution.py:61
  72.8 16.5 %attend.1 = (bf16[2,512,1088]{2,1,0:T(8,128)(2,1)}, bf16[2,512,960]{2,1,0:T(8,128)(2,1)}, f32[2,8,512]{2,1,0:T(8,128)}, bf16[2,512,320]{2,1,0:T(8,128)(2,1)}, f3...) custom-call(s32[3]{0:T(128)} %pad_add_fusion.3.place_ref, ...), custom_call_target="tpu_custom_call" | custom-call | flops 2852126720 | bytes 13369344 | tf_op jit(solution)/shard_map/attend/pallas_call | solution.py:272
  101.4 11.2 %collective-permute-done.22 = bf16[6,16,1088]{2,1,0:T(8,128)(2,1)S(1)} collective-permute-done((bf16[6,16,1088]{2,1,0:T(8,128)(2,1)S(1)}, bf16[6,16,1088]{2,1,0:T(8,128)(2,1)S(1)}, u32[]{:S(2)}, u32[]{:S(2)}) %collective-permute-start.22) | collective-permute-done | bytes 208928 | tf_op jit(solution)/shard_map/ppermute | solution.py:61
  114.6 3.3 %middle_rows.1 = (f32[2,128,1088]{2,1,0:T(8,128)}, bf16[2,128,1088]{2,1,0:T(8,128)(2,1)}) custom-call(bf16[2,128,1088]{2,1,0:T(8,128)(2,1)} %copy-done.2, f32[2,128,1088]{2,1,0:T(8,128)} %get-tuple-element.279.keep_ref, bf16[2,256,1088]{2,1,0:T(8,128)(2,1)} %bitcast.192, bf16[2,128,1088]{2,1,0:T(8,128)(2,1)} %bitcast.233, f32[8,1088]{1,0:T(8,128)} %get-tuple-element.282.vec_ref), custom_call_target="tpu_custom_call" | custom-call | tf_op jit(solution)/shard_map/middle_rows/pallas_call | solution.py:315
  125.2 6.1 %collective-permute-done.29 = bf16[4,16,1088]{2,1,0:T(8,128)(2,1)S(1)} collective-permute-done((bf16[4,16,1088]{2,1,0:T(8,128)(2,1)S(1)}, bf16[4,16,1088]{2,1,0:T(8,128)(2,1)S(1)}, u32[]{:S(2)}, u32[]{:S(2)}) %collective-permute-start.29) | collective-permute-done | bytes 139296 | tf_op jit(solution)/shard_map/ppermute | solution.py:61
  134.1 7.7 %feed_pull.1.pull_ref = bf16[2,512,1088]{2,1,0:T(8,128)(2,1)} custom-call(bf16[2,128,1088]{2,1,0:T(8,128)(2,1)} %copy-done.1, bf16[2,128,1088]{2,1,0:T(8,128)(2,1)} %bitcast.206, bf16[2,128,1088]{2,1,0:T(8,128)(2,1)} %bitcast.209, bf16[2,128,1088]{2,1,0:T(8,128)(2,1)} %bitcast.212, bf16[64,1088]{1,0:T(8,128)(2,1)} %bitcast.314, bf16[96,1088]{1,0:T(8,128)(2,1)} %bitcast.309, ...), custom_call_target="tpu_custom_call" | custom-call | flops 2424307712 | bytes 8912896 | tf_op jit(solution)/shard_map/feed_pull/pallas_call | solution.py:364
  143.2 14.6 %feed_forward.1 = (bf16[2,512,1088]{2,1,0:T(8,128)(2,1)}, bf16[2,512,1088]{2,1,0:T(8,128)(2,1)}, f32[2,128,1088]{2,1,0:T(8,128)}, bf16[2,128,1088]{2,1,0:T(8,128...) custom-call(bf16[2,128,1088]{2,1,0:T(8,128)(2,1)} %get-tuple-element.305.x0, bf16[2,128,1088]{2,1,0:T(8,128)(2,1)} %bitcast.217, ...), custom_call_target="tpu_custom_call" | custom-call | flops 4848615424 | bytes 13369344 | tf_op jit(solution)/shard_map/feed_forward/pallas_call | solution.py:415
  157.9 5.1 %feed_grads_first.1 = (bf16[112,1088]{1,0:T(8,128)(2,1)}, bf16[160,1088]{1,0:T(8,128)(2,1)}) custom-call(bf16[1024,1088]{1,0:T(8,128)(2,1)} %bitcast.193, bf16[1024,1088]{1,0:T(8,128)(2,1)} %bitcast.195, bf16[2,128,1088]{2,1,0:T(8,128)(2,1)} %copy-done.1, bf16[2,128,1088]{2,1,0:T(8,128)(2,1)} %bitcast.207, bf16[2,128,1088]{2,1,0:T(8,128)(2,1)} %bitcast.210, ...), custom_call_target="tpu_custom_call" | custom-call | flops 606076928 | bytes 8912896 | tf_op jit(solution)/shard_map/feed_grads_first/pallas_call | solution.py:549
  166.3 12.3 %feed_grads.1 = (bf16[272,1088]{1,0:T(8,128)(2,1)}, bf16[272,1088]{1,0:T(8,128)(2,1)}, bf16[272,1088]{1,0:T(8,128)(2,1)}, bf16[272,1088]{1,0:T(8,128)(2,1)}, bf1...) custom-call(bf16[1024,1088]{1,0:T(8,128)(2,1)} %bitcast.194, ...), custom_call_target="tpu_custom_call" | custom-call | flops 4848615424 | bytes 13369344 | tf_op jit(solution)/shard_map/feed_grads/pallas_call | solution.py:500
  181.9 4.2 %middle_pull.1 = (f32[2,128,1088]{2,1,0:T(8,128)}, bf16[2,128,1088]{2,1,0:T(8,128)(2,1)}, f32[4,1088]{1,0:T(4,128)}) custom-call(bf16[2,128,1088]{2,1,0:T(8,128)(2,1)} %copy-done.1, f32[2,128,1088]{2,1,0:T(8,128)} %get-tuple-element.288.middle_ref, f32[2,128,1088]{2,1,0:T(8,128)} %get-tuple-element.326.keep_ref, bf16[2,256,1088]{2,1,0:T(8,128)(2,1)} %bitcast.190, ...), custom_call_target="tpu_custom_call" | custom-call | tf_op jit(solution)/shard_map/middle_pull/pallas_call | solution.py:587
  190.0 7.6 %feed_out.1 = (f32[2,128,1088]{2,1,0:T(8,128)}, bf16[2,128,1088]{2,1,0:T(8,128)(2,1)}, bf16[2,256,1088]{2,1,0:T(8,128)(2,1)}) custom-call(bf16[2,512,1088]{2,1,0:T(8,128)(2,1)} %get-tuple-element.340.active_ref, bf16[64,1088]{1,0:T(8,128)(2,1)} %bitcast.315, bf16[96,1088]{1,0:T(8,128)(2,1)} %bitcast.311, bf16[64,1088]{1,0:T(8,128)(2,1)} %bitcast.313, ...), custom_call_target="tpu_custom_call" | custom-call | flops 2424307712 | bytes 8912896 | tf_op jit(solution)/shard_map/feed_out/pallas_call | solution.py:450
  197.6 4.4 %collective-permute-done.39 = bf16[7,16,1088]{2,1,0:T(8,128)(2,1)S(1)} collective-permute-done((bf16[7,16,1088]{2,1,0:T(8,128)(2,1)S(1)}, bf16[7,16,1088]{2,1,0:T(8,128)(2,1)S(1)}, u32[]{:S(2)}, u32[]{:S(2)}) %collective-permute-start.39) | collective-permute-done | bytes 243744 | tf_op jit(solution)/shard_map/ppermute | solution.py:61
  212.9 24.5 %attend_pull.1 = (f32[2,128,1088]{2,1,0:T(8,128)}, bf16[2,128,1088]{2,1,0:T(8,128)(2,1)}, bf16[2,256,1088]{2,1,0:T(8,128)(2,1)}, bf16[160,1088]{1,0:T(8,128)(2,1...) custom-call(s32[3]{0:T(128)} %pad_add_fusion.3.place_ref, ...), custom_call_target="tpu_custom_call" | custom-call | flops 7130316800 | bytes 13369344 | tf_op jit(solution)/shard_map/attend_pull/pallas_call | solution.py:680
  237.4 4.5 %collective-permute-done.43 = bf16[10,16,1088]{2,1,0:T(8,128)(2,1)S(1)} collective-permute-done((bf16[10,16,1088]{2,1,0:T(8,128)(2,1)S(1)}, bf16[10,16,1088]{2,1,0:T(8,128)(2,1)S(1)}, u32[]{:S(2)}, u32[]{:S(2)}) %collective-permute-start.43) | collective-permute-done | bytes 348192 | tf_op jit(solution)/shard_map/ppermute | solution.py:61
  252.1 5.6 %collective-permute-done.50 = bf16[10,16,1088]{2,1,0:T(8,128)(2,1)S(1)} collective-permute-done((bf16[10,16,1088]{2,1,0:T(8,128)(2,1)S(1)}, bf16[10,16,1088]{2,1,0:T(8,128)(2,1)S(1)}, u32[]{:S(2)}, u32[]{:S(2)}) %collective-permute-start.50) | collective-permute-done | bytes 348192 | tf_op jit(solution)/shard_map/ppermute | solution.py:61
  258.6 6.6 %collective-permute-done.51 = bf16[10,16,1088]{2,1,0:T(8,128)(2,1)S(1)} collective-permute-done((bf16[10,16,1088]{2,1,0:T(8,128)(2,1)S(1)}, bf16[10,16,1088]{2,1,0:T(8,128)(2,1)S(1)}, u32[]{:S(2)}, u32[]{:S(2)}) %collective-permute-start.51) | collective-permute-done | bytes 348192 | tf_op jit(solution)/shard_map/ppermute | solution.py:61
  266.2 3.3 %collective-permute-start.52 = (bf16[10,16,1088]{2,1,0:T(8,128)(2,1)}, bf16[10,16,1088]{2,1,0:T(8,128)(2,1)}, u32[]{:S(2)}, u32[]{:S(2)}) collective-permute-start(bf16[10,16,1088]{2,1,0:T(8,128)(2,1)} %bitcast.119), channel_id=1, source_target_pairs={{8,0},{12,4},{16,8},{20,12},{24,16},{28,20},{0,24},{4,28},{9,1},{1... | collective-permute-start | bytes 1044488 | tf_op jit(solution)/shard_map/ppermute | solution.py:61
  271.5 4.1 %input_pull.1 = (bf16[2,1088,128]{2,1,0:T(8,128)(2,1)}, f32[2,1088]{1,0:T(2,128)}) custom-call(bf16[2,128,1088]{2,1,0:T(8,128)(2,1)} %copy-done.2, f32[2,128,1088]{2,1,0:T(8,128)} %get-tuple-element.399.grad_ref, f32[2,128,1088]{2,1,0:T(8,128)} %get-tuple-element.400.keep_ref, bf16[2,256,1088]{2,1,0:T(8,128)(2,1)} %bitcast.188, ...), custom_call_target="tpu_custom_call" | custom-call | tf_op jit(solution)/shard_map/input_pull/pallas_call | solution.py:727
  283.2 8.4 %collective-permute-done.53 = bf16[10,16,1088]{2,1,0:T(8,128)(2,1)} collective-permute-done((bf16[10,16,1088]{2,1,0:T(8,128)(2,1)}, bf16[10,16,1088]{2,1,0:T(8,128)(2,1)}, u32[]{:S(2)}, u32[]{:S(2)}) %collective-permute-start.53) | collective-permute-done | bytes 348192 | tf_op jit(solution)/shard_map/ppermute | solution.py:61
  299.2 3.1 mixed_rows.1
  302.3 3.6 %collective-permute-done.57 = bf16[10,16,1088]{2,1,0:T(8,128)(2,1)S(1)} collective-permute-done((bf16[10,16,1088]{2,1,0:T(8,128)(2,1)}, bf16[10,16,1088]{2,1,0:T(8,128)(2,1)S(1)}, u32[]{:S(2)}, u32[]{:S(2)}) %collective-permute-start.57) | collective-permute-done | bytes 348192 | tf_op jit(solution)/shard_map/ppermute | solution.py:61
  (329 shorter events, 113.5 us)
Async XLA Ops:
  9.3 23.4 %collective-permute-start.6 = (bf16[2,8,16,1088]{3,2,1,0:T(8,128)(2,1)S(1)}, bf16[2,8,16,1088]{3,2,1,0:T(8,128)(2,1)}, u32[]{:S(2)}, u32[]{:S(2)}) collective-permute-start(bf16[2,8,16,1088]{3,2,1,0:T(8,128)(2,1)S(1)} %bitcast.183), channel_id=1, source_target_pairs={{0,2},{2,0},{1,3},{3,1},{4,6},{6,4},{5,7},{7,5},{8,10},{10,8},{9,1... | collective-permute-start | bytes 1671176 | tf_op jit(solution)/shard_map/ppermute | solution.py:61
  11.2 21.6 %collective-permute-start.3 = (bf16[11,16,1088]{2,1,0:T(8,128)(2,1)S(1)}, bf16[11,16,1088]{2,1,0:T(8,128)(2,1)S(1)}, u32[]{:S(2)}, u32[]{:S(2)}) collective-permute-start(bf16[11,16,1088]{2,1,0:T(8,128)(2,1)S(1)} %bitcast.235), channel_id=1, source_target_pairs={{0,8},{4,12},{8,16},{12,20},{16,24},{20,28},{24,0},{28,4},{1,9},{5... | collective-permute-start | bytes 1148936 | tf_op jit(solution)/shard_map/ppermute | solution.py:61
  12.7 20.0 %collective-permute-start.4 = (bf16[11,16,1088]{2,1,0:T(8,128)(2,1)S(1)}, bf16[11,16,1088]{2,1,0:T(8,128)(2,1)}, u32[]{:S(2)}, u32[]{:S(2)}) collective-permute-start(bf16[11,16,1088]{2,1,0:T(8,128)(2,1)S(1)} %bitcast.236), channel_id=1, source_target_pairs={{0,24},{4,28},{8,0},{12,4},{16,8},{20,12},{24,16},{28,20},{1,25},{... | collective-permute-start | bytes 1148936 | tf_op jit(solution)/shard_map/ppermute | solution.py:61
  15.0 17.8 %collective-permute-start.5 = (bf16[11,16,1088]{2,1,0:T(8,128)(2,1)S(1)}, bf16[11,16,1088]{2,1,0:T(8,128)(2,1)}, u32[]{:S(2)}, u32[]{:S(2)}) collective-permute-start(bf16[11,16,1088]{2,1,0:T(8,128)(2,1)S(1)} %bitcast.237), channel_id=1, source_target_pairs={{0,4},{4,0},{8,12},{12,8},{16,20},{20,16},{24,28},{28,24},{1,5},{5... | collective-permute-start | bytes 1148936 | tf_op jit(solution)/shard_map/ppermute | solution.py:61
  15.6 17.1 %collective-permute-start.7 = (bf16[9,16,1088]{2,1,0:T(8,128)(2,1)S(1)}, bf16[9,16,1088]{2,1,0:T(8,128)(2,1)}, u32[]{:S(2)}, u32[]{:S(2)}) collective-permute-start(bf16[9,16,1088]{2,1,0:T(8,128)(2,1)S(1)} %bitcast.243), channel_id=1, source_target_pairs={{0,4},{4,0},{8,12},{12,8},{16,20},{20,16},{24,28},{28,24},{1,5},{5... | collective-permute-start | bytes 940040 | tf_op jit(solution)/shard_map/ppermute | solution.py:61
  32.8 20.1 %collective-permute-start.11 = (bf16[2,8,16,1088]{3,2,1,0:T(8,128)(2,1)S(1)}, bf16[2,8,16,1088]{3,2,1,0:T(8,128)(2,1)S(1)}, u32[]{:S(2)}, u32[]{:S(2)}) collective-permute-start(bf16[2,8,16,1088]{3,2,1,0:T(8,128)(2,1)S(1)} %bitcast.181), channel_id=1, source_target_pairs={{0,2},{2,0},{1,3},{3,1},{4,6},{6,4},{5,7},{7,5},{8,10},{10,8},{9,1... | collective-permute-start | bytes 1671176 | tf_op jit(solution)/shard_map/ppermute | solution.py:61
  33.4 19.4 %collective-permute-start.8 = (bf16[11,16,1088]{2,1,0:T(8,128)(2,1)S(1)}, bf16[11,16,1088]{2,1,0:T(8,128)(2,1)S(1)}, u32[]{:S(2)}, u32[]{:S(2)}) collective-permute-start(bf16[11,16,1088]{2,1,0:T(8,128)(2,1)S(1)} %bitcast.238), channel_id=1, source_target_pairs={{0,16},{4,20},{8,24},{12,28},{16,0},{20,4},{24,8},{28,12},{1,17},{... | collective-permute-start | bytes 1148936 | tf_op jit(solution)/shard_map/ppermute | solution.py:61
  34.1 18.7 %collective-permute-start.9 = (bf16[11,16,1088]{2,1,0:T(8,128)(2,1)S(1)}, bf16[11,16,1088]{2,1,0:T(8,128)(2,1)S(1)}, u32[]{:S(2)}, u32[]{:S(2)}) collective-permute-start(bf16[11,16,1088]{2,1,0:T(8,128)(2,1)S(1)} %collective-permute-done.3), channel_id=1, source_target_pairs={{0,4},{4,0},{8,12},{12,8},{16,20},{20,16},{24,28},{28,24},{1,5},{5... | collective-permute-start | bytes 1148936 | tf_op jit(solution)/shard_map/ppermute | solution.py:61
  35.5 17.3 %collective-permute-start.10 = (bf16[11,16,1088]{2,1,0:T(8,128)(2,1)}, bf16[11,16,1088]{2,1,0:T(8,128)(2,1)S(1)}, u32[]{:S(2)}, u32[]{:S(2)}) collective-permute-start(bf16[11,16,1088]{2,1,0:T(8,128)(2,1)} %bitcast.25), channel_id=1, source_target_pairs={{0,4},{4,0},{8,12},{12,8},{16,20},{20,16},{24,28},{28,24},{1,5},{5... | collective-permute-start | bytes 1148936 | tf_op jit(solution)/shard_map/ppermute | solution.py:61
  52.8 16.7 %collective-permute-start.15 = (bf16[17,16,1088]{2,1,0:T(8,128)(2,1)S(1)}, bf16[17,16,1088]{2,1,0:T(8,128)(2,1)S(1)}, u32[]{:S(2)}, u32[]{:S(2)}) collective-permute-start(bf16[17,16,1088]{2,1,0:T(8,128)(2,1)S(1)} %bitcast.179), channel_id=1, source_target_pairs={{0,8},{4,12},{8,16},{12,20},{16,24},{20,28},{24,0},{28,4},{1,9},{5... | collective-permute-start | bytes 1775624 | tf_op jit(solution)/shard_map/ppermute | solution.py:61
  69.5 21.1 %collective-permute-start.17 = (bf16[17,16,1088]{2,1,0:T(8,128)(2,1)S(1)}, bf16[17,16,1088]{2,1,0:T(8,128)(2,1)S(1)}, u32[]{:S(2)}, u32[]{:S(2)}) collective-permute-start(bf16[17,16,1088]{2,1,0:T(8,128)(2,1)S(1)} %bitcast.180), channel_id=1, source_target_pairs={{0,24},{4,28},{8,0},{12,4},{16,8},{20,12},{24,16},{28,20},{1,25},{... | collective-permute-start | bytes 1775624 | tf_op jit(solution)/shard_map/ppermute | solution.py:61
  70.5 20.1 %collective-permute-start.18 = (bf16[17,16,1088]{2,1,0:T(8,128)(2,1)S(1)}, bf16[17,16,1088]{2,1,0:T(8,128)(2,1)S(1)}, u32[]{:S(2)}, u32[]{:S(2)}) collective-permute-start(bf16[17,16,1088]{2,1,0:T(8,128)(2,1)S(1)} %collective-permute-done.15), channel_id=1, source_target_pairs={{0,4},{4,0},{8,12},{12,8},{16,20},{20,16},{24,28},{28,24},{1,5},{5... | collective-permute-start | bytes 1775624 | tf_op jit(solution)/shard_map/ppermute | solution.py:61
  72.1 18.5 %collective-permute-start.19 = (bf16[8,16,1088]{2,1,0:T(8,128)(2,1)S(1)}, bf16[8,16,1088]{2,1,0:T(8,128)(2,1)S(1)}, u32[]{:S(2)}, u32[]{:S(2)}) collective-permute-start(bf16[8,16,1088]{2,1,0:T(8,128)(2,1)S(1)} %bitcast.245), channel_id=1, source_target_pairs={{0,4},{4,0},{8,12},{12,8},{16,20},{20,16},{24,28},{28,24},{1,5},{5... | collective-permute-start | bytes 835592 | tf_op jit(solution)/shard_map/ppermute | solution.py:61
  72.7 16.6 %collective-permute-start.16 = (bf16[4,16,1088]{2,1,0:T(8,128)(2,1)S(1)}, bf16[4,16,1088]{2,1,0:T(8,128)(2,1)S(1)}, u32[]{:S(2)}, u32[]{:S(2)}) collective-permute-start(bf16[4,16,1088]{2,1,0:T(8,128)(2,1)S(1)} %bitcast.251), channel_id=1, source_target_pairs={{0,16},{4,20},{8,24},{12,28},{16,0},{20,4},{24,8},{28,12},{1,17},{... | collective-permute-start | bytes 417800 | tf_op jit(solution)/shard_map/ppermute | solution.py:61
  95.4 18.3 %collective-permute-start.23 = (bf16[17,16,1088]{2,1,0:T(8,128)(2,1)S(1)}, bf16[17,16,1088]{2,1,0:T(8,128)(2,1)S(1)}, u32[]{:S(2)}, u32[]{:S(2)}) collective-permute-start(bf16[17,16,1088]{2,1,0:T(8,128)(2,1)S(1)} %collective-permute-done.17), channel_id=1, source_target_pairs={{0,4},{4,0},{8,12},{12,8},{16,20},{20,16},{24,28},{28,24},{1,5},{5... | collective-permute-start | bytes 1775624 | tf_op jit(solution)/shard_map/ppermute | solution.py:61
  163.1 17.5 %collective-permute-start.34 = (bf16[2,8,16,1088]{3,2,1,0:T(8,128)(2,1)S(1)}, bf16[2,8,16,1088]{3,2,1,0:T(8,128)(2,1)S(1)}, u32[]{:S(2)}, u32[]{:S(2)}) collective-permute-start(bf16[2,8,16,1088]{3,2,1,0:T(8,128)(2,1)S(1)} %bitcast.227), channel_id=1, source_target_pairs={{0,2},{2,0},{1,3},{3,1},{4,6},{6,4},{5,7},{7,5},{8,10},{10,8},{9,1... | collective-permute-start | bytes 1671176 | tf_op jit(solution)/shard_map/ppermute | solution.py:61
  208.8 33.1 %collective-permute-start.43 = (bf16[10,16,1088]{2,1,0:T(8,128)(2,1)S(1)}, bf16[10,16,1088]{2,1,0:T(8,128)(2,1)S(1)}, u32[]{:S(2)}, u32[]{:S(2)}) collective-permute-start(bf16[10,16,1088]{2,1,0:T(8,128)(2,1)S(1)} %bitcast.241), channel_id=1, source_target_pairs={{16,0},{20,4},{24,8},{28,12},{0,16},{4,20},{8,24},{12,28},{17,1},{... | collective-permute-start | bytes 1044488 | tf_op jit(solution)/shard_map/ppermute | solution.py:61
  210.6 31.3 %collective-permute-start.44 = (bf16[17,16,1088]{2,1,0:T(8,128)(2,1)}, bf16[17,16,1088]{2,1,0:T(8,128)(2,1)S(1)}, u32[]{:S(2)}, u32[]{:S(2)}) collective-permute-start(bf16[17,16,1088]{2,1,0:T(8,128)(2,1)} %bitcast.103), channel_id=1, source_target_pairs={{24,0},{28,4},{0,8},{4,12},{8,16},{12,20},{16,24},{20,28},{25,1},{... | collective-permute-start | bytes 1775624 | tf_op jit(solution)/shard_map/ppermute | solution.py:61
  210.8 31.1 %collective-permute-start.45 = (bf16[17,16,1088]{2,1,0:T(8,128)(2,1)}, bf16[17,16,1088]{2,1,0:T(8,128)(2,1)S(1)}, u32[]{:S(2)}, u32[]{:S(2)}) collective-permute-start(bf16[17,16,1088]{2,1,0:T(8,128)(2,1)} %bitcast.105), channel_id=1, source_target_pairs={{0,4},{4,0},{8,12},{12,8},{16,20},{20,16},{24,28},{28,24},{1,5},{5... | collective-permute-start | bytes 1775624 | tf_op jit(solution)/shard_map/ppermute | solution.py:61
  212.4 29.5 %collective-permute-start.46 = (bf16[17,16,1088]{2,1,0:T(8,128)(2,1)}, bf16[17,16,1088]{2,1,0:T(8,128)(2,1)S(1)}, u32[]{:S(2)}, u32[]{:S(2)}) collective-permute-start(bf16[17,16,1088]{2,1,0:T(8,128)(2,1)} %bitcast.107), channel_id=1, source_target_pairs={{0,4},{4,0},{8,12},{12,8},{16,20},{20,16},{24,28},{28,24},{1,5},{5... | collective-permute-start | bytes 1775624 | tf_op jit(solution)/shard_map/ppermute | solution.py:61
  249.0 17.2 %collective-permute-start.48 = (bf16[2,8,16,1088]{3,2,1,0:T(8,128)(2,1)S(1)}, bf16[2,8,16,1088]{3,2,1,0:T(8,128)(2,1)S(1)}, u32[]{:S(2)}, u32[]{:S(2)}) collective-permute-start(bf16[2,8,16,1088]{3,2,1,0:T(8,128)(2,1)S(1)} %bitcast.228), channel_id=1, source_target_pairs={{0,2},{2,0},{1,3},{3,1},{4,6},{6,4},{5,7},{7,5},{8,10},{10,8},{9,1... | collective-permute-start | bytes 1671176 | tf_op jit(solution)/shard_map/ppermute | solution.py:61
  266.2 17.1 %collective-permute-start.52 = (bf16[10,16,1088]{2,1,0:T(8,128)(2,1)}, bf16[10,16,1088]{2,1,0:T(8,128)(2,1)}, u32[]{:S(2)}, u32[]{:S(2)}) collective-permute-start(bf16[10,16,1088]{2,1,0:T(8,128)(2,1)} %bitcast.119), channel_id=1, source_target_pairs={{8,0},{12,4},{16,8},{20,12},{24,16},{28,20},{0,24},{4,28},{9,1},{1... | collective-permute-start | bytes 1044488 | tf_op jit(solution)/shard_map/ppermute | solution.py:61
  269.4 22.2 %collective-permute-start.53 = (bf16[10,16,1088]{2,1,0:T(8,128)(2,1)}, bf16[10,16,1088]{2,1,0:T(8,128)(2,1)}, u32[]{:S(2)}, u32[]{:S(2)}) collective-permute-start(bf16[10,16,1088]{2,1,0:T(8,128)(2,1)} %bitcast.121), channel_id=1, source_target_pairs={{16,0},{20,4},{24,8},{28,12},{0,16},{4,20},{8,24},{12,28},{17,1},{... | collective-permute-start | bytes 1044488 | tf_op jit(solution)/shard_map/ppermute | solution.py:61
  270.0 21.6 %collective-permute-start.55 = (bf16[10,16,1088]{2,1,0:T(8,128)(2,1)}, bf16[10,16,1088]{2,1,0:T(8,128)(2,1)}, u32[]{:S(2)}, u32[]{:S(2)}) collective-permute-start(bf16[10,16,1088]{2,1,0:T(8,128)(2,1)} %bitcast.125), channel_id=1, source_target_pairs={{0,4},{4,0},{8,12},{12,8},{16,20},{20,16},{24,28},{28,24},{1,5},{5... | collective-permute-start | bytes 1044488 | tf_op jit(solution)/shard_map/ppermute | solution.py:61
  (107 other events, 1334.1 us)

commit v3 on v2

--- a/solution.py
+++ b/solution.py
@@ -23,7 +23,7 @@
 ORDER = ((2, 1), (2, 0), (0, 0), (0, 1), (1, 0), (1, 1), (3, 0), (3, 1))
 THIRDS = (64, 160)
 CUT = 144
-BACK_CUT = 112
+BACK_CUT = 144
 SIDE_PAIRS = [(p, p ^ 1) for p in range(8)]
 
 

time: 322 us -> 320 us (level)
  transfers between devices with their start and end apart: 65 -> 65, of which waited for: 29 -> 29; matrix products, arithmetic and copies ran while one was open for 6% -> 7% of each run, Pallas kernels for 25% -> 26%
where the time goes in v3:
time: 320 us; the launch traced here: 316 us
  waiting for transfers between devices  116 us (36%)
  Pallas kernels  103 us (32%)
  starting transfers between devices  64.9 us (20%)
  other arithmetic  21.7 us (7%)
  local copies, waits for them, and re-layouts  9.5 us (3%)
    ppermute x55, waiting for transfers between devices, send(): return lax.ppermute(cut, axes, pairs).reshape(value.shape)  111 us
    ppermute x55, starting transfers between devices, send(): return lax.ppermute(cut, axes, pairs).reshape(value.shape)  54.8 us
    pallas_call x1, Pallas kernels, attend_pull(): pl.pallas_call(attend_pull_kernel, grid=(micro,), in_specs=[SCALARS] + [o...  24.7 us
    pallas_call x1, Pallas kernels, attend(): pl.pallas_call(attend_kernel, grid=(micro,), in_specs=[SCALARS] + [per((r...  16.4 us
    pallas_call x1, Pallas kernels, feed_forward(): pl.pallas_call(partial(feed_kernel, parts), grid=(micro,), in_specs=[per(...  14.4 us
    pallas_call x1, Pallas kernels, feed_grads(): pl.pallas_call(feed_grads_kernel, grid=(2,), in_specs=[whole(a) for a in...  12.2 us
    pallas_call x1, Pallas kernels, feed_pull(): pl.pallas_call(partial(pull_kernel, parts), grid=(micro,), in_specs=[per(...  7.73 us
    pallas_call x1, Pallas kernels, feed_out(): pl.pallas_call(partial(feed_out_kernel, parts), grid=(micro,), in_specs=[...  7.55 us
  transfers between devices with their start and end apart: 65, of which 29 were waited for; matrix products, arithmetic and copies ran while one was open for 7% of the time, Pallas kernels for 26%

profile of v3, /device:TPU:0, one launch (start us, length us, event | category | flops | bytes accessed | tf_op | source)
XLA Modules:
  0.0 316.1 jit_solution(6956914208880036783)
XLA Ops:
  17.5 15.3 %collective-permute-done.7 = bf16[9,16,1088]{2,1,0:T(8,128)(2,1)} collective-permute-done((bf16[9,16,1088]{2,1,0:T(8,128)(2,1)S(1)}, bf16[9,16,1088]{2,1,0:T(8,128)(2,1)}, u32[]{:S(2)}, u32[]{:S(2)}) %collective-permute-start.7) | collective-permute-done | bytes 313376 | tf_op jit(solution)/shard_map/ppermute | solution.py:61
  36.2 16.7 %collective-permute-done.8 = bf16[11,16,1088]{2,1,0:T(8,128)(2,1)S(1)} collective-permute-done((bf16[11,16,1088]{2,1,0:T(8,128)(2,1)S(1)}, bf16[11,16,1088]{2,1,0:T(8,128)(2,1)S(1)}, u32[]{:S(2)}, u32[]{:S(2)}) %collective-permute-start.8) | collective-permute-done | bytes 383008 | tf_op jit(solution)/shard_map/ppermute | solution.py:61
  55.8 9.9 %collective-permute-done.12 = bf16[11,16,1088]{2,1,0:T(8,128)(2,1)S(1)} collective-permute-done((bf16[11,16,1088]{2,1,0:T(8,128)(2,1)S(1)}, bf16[11,16,1088]{2,1,0:T(8,128)(2,1)S(1)}, u32[]{:S(2)}, u32[]{:S(2)}) %collective-permute-start.12) | collective-permute-done | bytes 383008 | tf_op jit(solution)/shard_map/ppermute | solution.py:61
  65.7 3.9 %collective-permute-done.15 = bf16[17,16,1088]{2,1,0:T(8,128)(2,1)S(1)} collective-permute-done((bf16[17,16,1088]{2,1,0:T(8,128)(2,1)S(1)}, bf16[17,16,1088]{2,1,0:T(8,128)(2,1)S(1)}, u32[]{:S(2)}, u32[]{:S(2)}) %collective-permute-start.15) | collective-permute-done | bytes 591904 | tf_op jit(solution)/shard_map/ppermute | solution.py:61
  72.9 16.4 %attend.1 = (bf16[2,512,1088]{2,1,0:T(8,128)(2,1)}, bf16[2,512,960]{2,1,0:T(8,128)(2,1)}, f32[2,8,512]{2,1,0:T(8,128)}, bf16[2,512,320]{2,1,0:T(8,128)(2,1)}, f3...) custom-call(s32[3]{0:T(128)} %pad_add_fusion.3.place_ref, ...), custom_call_target="tpu_custom_call" | custom-call | flops 2852126720 | bytes 13369344 | tf_op jit(solution)/shard_map/attend/pallas_call | solution.py:272
  90.8 3.0 collective-permute-done.20
  101.4 11.2 %collective-permute-done.22 = bf16[6,16,1088]{2,1,0:T(8,128)(2,1)S(1)} collective-permute-done((bf16[6,16,1088]{2,1,0:T(8,128)(2,1)S(1)}, bf16[6,16,1088]{2,1,0:T(8,128)(2,1)S(1)}, u32[]{:S(2)}, u32[]{:S(2)}) %collective-permute-start.22) | collective-permute-done | bytes 208928 | tf_op jit(solution)/shard_map/ppermute | solution.py:61
  114.6 3.3 %middle_rows.1 = (f32[2,128,1088]{2,1,0:T(8,128)}, bf16[2,128,1088]{2,1,0:T(8,128)(2,1)}) custom-call(bf16[2,128,1088]{2,1,0:T(8,128)(2,1)} %copy-done.2, f32[2,128,1088]{2,1,0:T(8,128)} %get-tuple-element.279.keep_ref, bf16[2,256,1088]{2,1,0:T(8,128)(2,1)} %bitcast.192, bf16[2,128,1088]{2,1,0:T(8,128)(2,1)} %bitcast.233, f32[8,1088]{1,0:T(8,128)} %get-tuple-element.282.vec_ref), custom_call_target="tpu_custom_call" | custom-call | tf_op jit(solution)/shard_map/middle_rows/pallas_call | solution.py:315
  125.2 6.1 %collective-permute-done.29 = bf16[4,16,1088]{2,1,0:T(8,128)(2,1)S(1)} collective-permute-done((bf16[4,16,1088]{2,1,0:T(8,128)(2,1)S(1)}, bf16[4,16,1088]{2,1,0:T(8,128)(2,1)S(1)}, u32[]{:S(2)}, u32[]{:S(2)}) %collective-permute-start.29) | collective-permute-done | bytes 139296 | tf_op jit(solution)/shard_map/ppermute | solution.py:61
  134.2 7.7 %feed_pull.1.pull_ref = bf16[2,512,1088]{2,1,0:T(8,128)(2,1)} custom-call(bf16[2,128,1088]{2,1,0:T(8,128)(2,1)} %copy-done.1, bf16[2,128,1088]{2,1,0:T(8,128)(2,1)} %bitcast.206, bf16[2,128,1088]{2,1,0:T(8,128)(2,1)} %bitcast.209, bf16[2,128,1088]{2,1,0:T(8,128)(2,1)} %bitcast.212, bf16[64,1088]{1,0:T(8,128)(2,1)} %bitcast.313, bf16[96,1088]{1,0:T(8,128)(2,1)} %bitcast.308, ...), custom_call_target="tpu_custom_call" | custom-call | flops 2424307712 | bytes 8912896 | tf_op jit(solution)/shard_map/feed_pull/pallas_call | solution.py:364
  143.4 14.4 %feed_forward.1 = (bf16[2,512,1088]{2,1,0:T(8,128)(2,1)}, bf16[2,512,1088]{2,1,0:T(8,128)(2,1)}, f32[2,128,1088]{2,1,0:T(8,128)}, bf16[2,128,1088]{2,1,0:T(8,128...) custom-call(bf16[2,128,1088]{2,1,0:T(8,128)(2,1)} %get-tuple-element.305.x0, bf16[2,128,1088]{2,1,0:T(8,128)(2,1)} %bitcast.217, ...), custom_call_target="tpu_custom_call" | custom-call | flops 4848615424 | bytes 13369344 | tf_op jit(solution)/shard_map/feed_forward/pallas_call | solution.py:415
  157.8 5.1 %feed_grads_first.1 = (bf16[144,1088]{1,0:T(8,128)(2,1)}, bf16[128,1088]{1,0:T(8,128)(2,1)}) custom-call(bf16[1024,1088]{1,0:T(8,128)(2,1)} %bitcast.193, bf16[1024,1088]{1,0:T(8,128)(2,1)} %bitcast.195, bf16[2,128,1088]{2,1,0:T(8,128)(2,1)} %copy-done.1, bf16[2,128,1088]{2,1,0:T(8,128)(2,1)} %bitcast.207, bf16[2,128,1088]{2,1,0:T(8,128)(2,1)} %bitcast.210, ...), custom_call_target="tpu_custom_call" | custom-call | flops 606076928 | bytes 8912896 | tf_op jit(solution)/shard_map/feed_grads_first/pallas_call | solution.py:549
  166.3 12.2 %feed_grads.1 = (bf16[272,1088]{1,0:T(8,128)(2,1)}, bf16[272,1088]{1,0:T(8,128)(2,1)}, bf16[272,1088]{1,0:T(8,128)(2,1)}, bf16[272,1088]{1,0:T(8,128)(2,1)}, bf1...) custom-call(bf16[1024,1088]{1,0:T(8,128)(2,1)} %bitcast.194, ...), custom_call_target="tpu_custom_call" | custom-call | flops 4848615424 | bytes 13369344 | tf_op jit(solution)/shard_map/feed_grads/pallas_call | solution.py:500
  181.8 4.1 %middle_pull.1 = (f32[2,128,1088]{2,1,0:T(8,128)}, bf16[2,128,1088]{2,1,0:T(8,128)(2,1)}, f32[4,1088]{1,0:T(4,128)}) custom-call(bf16[2,128,1088]{2,1,0:T(8,128)(2,1)} %copy-done.1, f32[2,128,1088]{2,1,0:T(8,128)} %get-tuple-element.288.middle_ref, f32[2,128,1088]{2,1,0:T(8,128)} %get-tuple-element.326.keep_ref, bf16[2,256,1088]{2,1,0:T(8,128)(2,1)} %bitcast.190, ...), custom_call_target="tpu_custom_call" | custom-call | tf_op jit(solution)/shard_map/middle_pull/pallas_call | solution.py:587
  191.6 7.6 %feed_out.1 = (f32[2,128,1088]{2,1,0:T(8,128)}, bf16[2,128,1088]{2,1,0:T(8,128)(2,1)}, bf16[2,256,1088]{2,1,0:T(8,128)(2,1)}) custom-call(bf16[2,512,1088]{2,1,0:T(8,128)(2,1)} %get-tuple-element.340.active_ref, bf16[64,1088]{1,0:T(8,128)(2,1)} %bitcast.314, bf16[96,1088]{1,0:T(8,128)(2,1)} %bitcast.310, bf16[64,1088]{1,0:T(8,128)(2,1)} %bitcast.312, ...), custom_call_target="tpu_custom_call" | custom-call | flops 2424307712 | bytes 8912896 | tf_op jit(solution)/shard_map/feed_out/pallas_call | solution.py:450
  199.2 5.9 %collective-permute-done.39 = bf16[9,16,1088]{2,1,0:T(8,128)(2,1)S(1)} collective-permute-done((bf16[9,16,1088]{2,1,0:T(8,128)(2,1)S(1)}, bf16[9,16,1088]{2,1,0:T(8,128)(2,1)S(1)}, u32[]{:S(2)}, u32[]{:S(2)}) %collective-permute-start.39) | collective-permute-done | bytes 313376 | tf_op jit(solution)/shard_map/ppermute | solution.py:61
  214.0 24.7 %attend_pull.1 = (f32[2,128,1088]{2,1,0:T(8,128)}, bf16[2,128,1088]{2,1,0:T(8,128)(2,1)}, bf16[2,256,1088]{2,1,0:T(8,128)(2,1)}, bf16[160,1088]{1,0:T(8,128)(2,1...) custom-call(s32[3]{0:T(128)} %pad_add_fusion.3.place_ref, ...), custom_call_target="tpu_custom_call" | custom-call | flops 7130316800 | bytes 13369344 | tf_op jit(solution)/shard_map/attend_pull/pallas_call | solution.py:680
  251.4 5.4 %collective-permute-done.50 = bf16[10,16,1088]{2,1,0:T(8,128)(2,1)S(1)} collective-permute-done((bf16[10,16,1088]{2,1,0:T(8,128)(2,1)S(1)}, bf16[10,16,1088]{2,1,0:T(8,128)(2,1)S(1)}, u32[]{:S(2)}, u32[]{:S(2)}) %collective-permute-start.50) | collective-permute-done | bytes 348192 | tf_op jit(solution)/shard_map/ppermute | solution.py:61
  257.6 6.2 %collective-permute-done.51 = bf16[10,16,1088]{2,1,0:T(8,128)(2,1)S(1)} collective-permute-done((bf16[10,16,1088]{2,1,0:T(8,128)(2,1)S(1)}, bf16[10,16,1088]{2,1,0:T(8,128)(2,1)S(1)}, u32[]{:S(2)}, u32[]{:S(2)}) %collective-permute-start.51) | collective-permute-done | bytes 348192 | tf_op jit(solution)/shard_map/ppermute | solution.py:61
  264.7 3.7 %collective-permute-start.52 = (bf16[10,16,1088]{2,1,0:T(8,128)(2,1)}, bf16[10,16,1088]{2,1,0:T(8,128)(2,1)}, u32[]{:S(2)}, u32[]{:S(2)}) collective-permute-start(bf16[10,16,1088]{2,1,0:T(8,128)(2,1)} %bitcast.119), channel_id=1, source_target_pairs={{8,0},{12,4},{16,8},{20,12},{24,16},{28,20},{0,24},{4,28},{9,1},{1... | collective-permute-start | bytes 1044488 | tf_op jit(solution)/shard_map/ppermute | solution.py:61
  270.4 4.0 %input_pull.1 = (bf16[2,1088,128]{2,1,0:T(8,128)(2,1)}, f32[2,1088]{1,0:T(2,128)}) custom-call(bf16[2,128,1088]{2,1,0:T(8,128)(2,1)} %copy-done.2, f32[2,128,1088]{2,1,0:T(8,128)} %get-tuple-element.399.grad_ref, f32[2,128,1088]{2,1,0:T(8,128)} %get-tuple-element.400.keep_ref, bf16[2,256,1088]{2,1,0:T(8,128)(2,1)} %bitcast.188, ...), custom_call_target="tpu_custom_call" | custom-call | tf_op jit(solution)/shard_map/input_pull/pallas_call | solution.py:727
  276.5 3.7 %collective-permute-done.54 = bf16[10,16,1088]{2,1,0:T(8,128)(2,1)} collective-permute-done((bf16[10,16,1088]{2,1,0:T(8,128)(2,1)}, bf16[10,16,1088]{2,1,0:T(8,128)(2,1)}, u32[]{:S(2)}, u32[]{:S(2)}) %collective-permute-start.54) | collective-permute-done | bytes 348192 | tf_op jit(solution)/shard_map/ppermute | solution.py:61
  282.2 8.6 %collective-permute-done.53 = bf16[10,16,1088]{2,1,0:T(8,128)(2,1)} collective-permute-done((bf16[10,16,1088]{2,1,0:T(8,128)(2,1)}, bf16[10,16,1088]{2,1,0:T(8,128)(2,1)}, u32[]{:S(2)}, u32[]{:S(2)}) %collective-permute-start.53) | collective-permute-done | bytes 348192 | tf_op jit(solution)/shard_map/ppermute | solution.py:61
  298.3 3.1 mixed_rows.1
  (327 shorter events, 112.1 us)
Async XLA Ops:
  9.3 23.5 %collective-permute-start.6 = (bf16[2,8,16,1088]{3,2,1,0:T(8,128)(2,1)S(1)}, bf16[2,8,16,1088]{3,2,1,0:T(8,128)(2,1)}, u32[]{:S(2)}, u32[]{:S(2)}) collective-permute-start(bf16[2,8,16,1088]{3,2,1,0:T(8,128)(2,1)S(1)} %bitcast.183), channel_id=1, source_target_pairs={{0,2},{2,0},{1,3},{3,1},{4,6},{6,4},{5,7},{7,5},{8,10},{10,8},{9,1... | collective-permute-start | bytes 1671176 | tf_op jit(solution)/shard_map/ppermute | solution.py:61
  11.2 21.6 %collective-permute-start.3 = (bf16[11,16,1088]{2,1,0:T(8,128)(2,1)S(1)}, bf16[11,16,1088]{2,1,0:T(8,128)(2,1)S(1)}, u32[]{:S(2)}, u32[]{:S(2)}) collective-permute-start(bf16[11,16,1088]{2,1,0:T(8,128)(2,1)S(1)} %bitcast.235), channel_id=1, source_target_pairs={{0,8},{4,12},{8,16},{12,20},{16,24},{20,28},{24,0},{28,4},{1,9},{5... | collective-permute-start | bytes 1148936 | tf_op jit(solution)/shard_map/ppermute | solution.py:61
  12.8 20.0 %collective-permute-start.4 = (bf16[11,16,1088]{2,1,0:T(8,128)(2,1)S(1)}, bf16[11,16,1088]{2,1,0:T(8,128)(2,1)}, u32[]{:S(2)}, u32[]{:S(2)}) collective-permute-start(bf16[11,16,1088]{2,1,0:T(8,128)(2,1)S(1)} %bitcast.236), channel_id=1, source_target_pairs={{0,24},{4,28},{8,0},{12,4},{16,8},{20,12},{24,16},{28,20},{1,25},{... | collective-permute-start | bytes 1148936 | tf_op jit(solution)/shard_map/ppermute | solution.py:61
  15.1 17.8 %collective-permute-start.5 = (bf16[11,16,1088]{2,1,0:T(8,128)(2,1)S(1)}, bf16[11,16,1088]{2,1,0:T(8,128)(2,1)}, u32[]{:S(2)}, u32[]{:S(2)}) collective-permute-start(bf16[11,16,1088]{2,1,0:T(8,128)(2,1)S(1)} %bitcast.237), channel_id=1, source_target_pairs={{0,4},{4,0},{8,12},{12,8},{16,20},{20,16},{24,28},{28,24},{1,5},{5... | collective-permute-start | bytes 1148936 | tf_op jit(solution)/shard_map/ppermute | solution.py:61
  15.7 17.1 %collective-permute-start.7 = (bf16[9,16,1088]{2,1,0:T(8,128)(2,1)S(1)}, bf16[9,16,1088]{2,1,0:T(8,128)(2,1)}, u32[]{:S(2)}, u32[]{:S(2)}) collective-permute-start(bf16[9,16,1088]{2,1,0:T(8,128)(2,1)S(1)} %bitcast.241), channel_id=1, source_target_pairs={{0,4},{4,0},{8,12},{12,8},{16,20},{20,16},{24,28},{28,24},{1,5},{5... | collective-permute-start | bytes 940040 | tf_op jit(solution)/shard_map/ppermute | solution.py:61
  32.8 20.1 %collective-permute-start.11 = (bf16[2,8,16,1088]{3,2,1,0:T(8,128)(2,1)S(1)}, bf16[2,8,16,1088]{3,2,1,0:T(8,128)(2,1)S(1)}, u32[]{:S(2)}, u32[]{:S(2)}) collective-permute-start(bf16[2,8,16,1088]{3,2,1,0:T(8,128)(2,1)S(1)} %bitcast.181), channel_id=1, source_target_pairs={{0,2},{2,0},{1,3},{3,1},{4,6},{6,4},{5,7},{7,5},{8,10},{10,8},{9,1... | collective-permute-start | bytes 1671176 | tf_op jit(solution)/shard_map/ppermute | solution.py:61
  33.4 19.4 %collective-permute-start.8 = (bf16[11,16,1088]{2,1,0:T(8,128)(2,1)S(1)}, bf16[11,16,1088]{2,1,0:T(8,128)(2,1)S(1)}, u32[]{:S(2)}, u32[]{:S(2)}) collective-permute-start(bf16[11,16,1088]{2,1,0:T(8,128)(2,1)S(1)} %bitcast.238), channel_id=1, source_target_pairs={{0,16},{4,20},{8,24},{12,28},{16,0},{20,4},{24,8},{28,12},{1,17},{... | collective-permute-start | bytes 1148936 | tf_op jit(solution)/shard_map/ppermute | solution.py:61
  34.2 18.7 %collective-permute-start.9 = (bf16[11,16,1088]{2,1,0:T(8,128)(2,1)S(1)}, bf16[11,16,1088]{2,1,0:T(8,128)(2,1)S(1)}, u32[]{:S(2)}, u32[]{:S(2)}) collective-permute-start(bf16[11,16,1088]{2,1,0:T(8,128)(2,1)S(1)} %collective-permute-done.3), channel_id=1, source_target_pairs={{0,4},{4,0},{8,12},{12,8},{16,20},{20,16},{24,28},{28,24},{1,5},{5... | collective-permute-start | bytes 1148936 | tf_op jit(solution)/shard_map/ppermute | solution.py:61
  35.5 17.3 %collective-permute-start.10 = (bf16[11,16,1088]{2,1,0:T(8,128)(2,1)}, bf16[11,16,1088]{2,1,0:T(8,128)(2,1)S(1)}, u32[]{:S(2)}, u32[]{:S(2)}) collective-permute-start(bf16[11,16,1088]{2,1,0:T(8,128)(2,1)} %bitcast.25), channel_id=1, source_target_pairs={{0,4},{4,0},{8,12},{12,8},{16,20},{20,16},{24,28},{28,24},{1,5},{5... | collective-permute-start | bytes 1148936 | tf_op jit(solution)/shard_map/ppermute | solution.py:61
  69.6 21.1 %collective-permute-start.17 = (bf16[17,16,1088]{2,1,0:T(8,128)(2,1)S(1)}, bf16[17,16,1088]{2,1,0:T(8,128)(2,1)S(1)}, u32[]{:S(2)}, u32[]{:S(2)}) collective-permute-start(bf16[17,16,1088]{2,1,0:T(8,128)(2,1)S(1)} %bitcast.180), channel_id=1, source_target_pairs={{0,24},{4,28},{8,0},{12,4},{16,8},{20,12},{24,16},{28,20},{1,25},{... | collective-permute-start | bytes 1775624 | tf_op jit(solution)/shard_map/ppermute | solution.py:61
  70.6 20.1 %collective-permute-start.18 = (bf16[17,16,1088]{2,1,0:T(8,128)(2,1)S(1)}, bf16[17,16,1088]{2,1,0:T(8,128)(2,1)S(1)}, u32[]{:S(2)}, u32[]{:S(2)}) collective-permute-start(bf16[17,16,1088]{2,1,0:T(8,128)(2,1)S(1)} %collective-permute-done.15), channel_id=1, source_target_pairs={{0,4},{4,0},{8,12},{12,8},{16,20},{20,16},{24,28},{28,24},{1,5},{5... | collective-permute-start | bytes 1775624 | tf_op jit(solution)/shard_map/ppermute | solution.py:61
  72.2 18.5 %collective-permute-start.19 = (bf16[8,16,1088]{2,1,0:T(8,128)(2,1)S(1)}, bf16[8,16,1088]{2,1,0:T(8,128)(2,1)S(1)}, u32[]{:S(2)}, u32[]{:S(2)}) collective-permute-start(bf16[8,16,1088]{2,1,0:T(8,128)(2,1)S(1)} %bitcast.247), channel_id=1, source_target_pairs={{0,4},{4,0},{8,12},{12,8},{16,20},{20,16},{24,28},{28,24},{1,5},{5... | collective-permute-start | bytes 835592 | tf_op jit(solution)/shard_map/ppermute | solution.py:61
  95.5 18.3 %collective-permute-start.23 = (bf16[17,16,1088]{2,1,0:T(8,128)(2,1)S(1)}, bf16[17,16,1088]{2,1,0:T(8,128)(2,1)S(1)}, u32[]{:S(2)}, u32[]{:S(2)}) collective-permute-start(bf16[17,16,1088]{2,1,0:T(8,128)(2,1)S(1)} %collective-permute-done.17), channel_id=1, source_target_pairs={{0,4},{4,0},{8,12},{12,8},{16,20},{20,16},{24,28},{28,24},{1,5},{5... | collective-permute-start | bytes 1775624 | tf_op jit(solution)/shard_map/ppermute | solution.py:61
  163.1 17.4 %collective-permute-start.34 = (bf16[2,8,16,1088]{3,2,1,0:T(8,128)(2,1)S(1)}, bf16[2,8,16,1088]{3,2,1,0:T(8,128)(2,1)S(1)}, u32[]{:S(2)}, u32[]{:S(2)}) collective-permute-start(bf16[2,8,16,1088]{3,2,1,0:T(8,128)(2,1)S(1)} %bitcast.227), channel_id=1, source_target_pairs={{0,2},{2,0},{1,3},{3,1},{4,6},{6,4},{5,7},{7,5},{8,10},{10,8},{9,1... | collective-permute-start | bytes 1671176 | tf_op jit(solution)/shard_map/ppermute | solution.py:61
  186.0 19.1 %collective-permute-start.37 = (bf16[2,8,16,1088]{3,2,1,0:T(8,128)(2,1)}, bf16[2,8,16,1088]{3,2,1,0:T(8,128)(2,1)S(1)}, u32[]{:S(2)}, u32[]{:S(2)}) collective-permute-start(bf16[2,8,16,1088]{3,2,1,0:T(8,128)(2,1)} %bitcast.280), channel_id=1, source_target_pairs={{0,2},{2,0},{1,3},{3,1},{4,6},{6,4},{5,7},{7,5},{8,10},{10,8},{9,1... | collective-permute-start | bytes 1671176 | tf_op jit(solution)/shard_map/ppermute | solution.py:61
  187.1 17.9 %collective-permute-start.38 = (bf16[2,8,16,1088]{3,2,1,0:T(8,128)(2,1)}, bf16[2,8,16,1088]{3,2,1,0:T(8,128)(2,1)S(1)}, u32[]{:S(2)}, u32[]{:S(2)}) collective-permute-start(bf16[2,8,16,1088]{3,2,1,0:T(8,128)(2,1)} %bitcast.281), channel_id=1, source_target_pairs={{0,1},{1,0},{2,3},{3,2},{4,5},{5,4},{6,7},{7,6},{8,9},{9,8},{10,11... | collective-permute-start | bytes 1671176 | tf_op jit(solution)/shard_map/ppermute | solution.py:61
  187.2 17.9 %collective-permute-start.39 = (bf16[9,16,1088]{2,1,0:T(8,128)(2,1)S(1)}, bf16[9,16,1088]{2,1,0:T(8,128)(2,1)S(1)}, u32[]{:S(2)}, u32[]{:S(2)}) collective-permute-start(bf16[9,16,1088]{2,1,0:T(8,128)(2,1)S(1)} %bitcast.242), channel_id=1, source_target_pairs={{16,0},{20,4},{24,8},{28,12},{0,16},{4,20},{8,24},{12,28},{17,1},{... | collective-permute-start | bytes 940040 | tf_op jit(solution)/shard_map/ppermute | solution.py:61
  209.1 29.9 %collective-permute-start.43 = (bf16[8,16,1088]{2,1,0:T(8,128)(2,1)}, bf16[8,16,1088]{2,1,0:T(8,128)(2,1)S(1)}, u32[]{:S(2)}, u32[]{:S(2)}) collective-permute-start(bf16[8,16,1088]{2,1,0:T(8,128)(2,1)} %bitcast.101), channel_id=1, source_target_pairs={{16,0},{20,4},{24,8},{28,12},{0,16},{4,20},{8,24},{12,28},{17,1},{... | collective-permute-start | bytes 835592 | tf_op jit(solution)/shard_map/ppermute | solution.py:61
  210.2 28.8 %collective-permute-start.44 = (bf16[17,16,1088]{2,1,0:T(8,128)(2,1)}, bf16[17,16,1088]{2,1,0:T(8,128)(2,1)S(1)}, u32[]{:S(2)}, u32[]{:S(2)}) collective-permute-start(bf16[17,16,1088]{2,1,0:T(8,128)(2,1)} %bitcast.103), channel_id=1, source_target_pairs={{24,0},{28,4},{0,8},{4,12},{8,16},{12,20},{16,24},{20,28},{25,1},{... | collective-permute-start | bytes 1775624 | tf_op jit(solution)/shard_map/ppermute | solution.py:61
  211.9 27.1 %collective-permute-start.45 = (bf16[17,16,1088]{2,1,0:T(8,128)(2,1)}, bf16[17,16,1088]{2,1,0:T(8,128)(2,1)S(1)}, u32[]{:S(2)}, u32[]{:S(2)}) collective-permute-start(bf16[17,16,1088]{2,1,0:T(8,128)(2,1)} %bitcast.105), channel_id=1, source_target_pairs={{0,4},{4,0},{8,12},{12,8},{16,20},{20,16},{24,28},{28,24},{1,5},{5... | collective-permute-start | bytes 1775624 | tf_op jit(solution)/shard_map/ppermute | solution.py:61
  213.6 27.6 %collective-permute-start.46 = (bf16[17,16,1088]{2,1,0:T(8,128)(2,1)}, bf16[17,16,1088]{2,1,0:T(8,128)(2,1)S(1)}, u32[]{:S(2)}, u32[]{:S(2)}) collective-permute-start(bf16[17,16,1088]{2,1,0:T(8,128)(2,1)} %bitcast.107), channel_id=1, source_target_pairs={{0,4},{4,0},{8,12},{12,8},{16,20},{20,16},{24,28},{28,24},{1,5},{5... | collective-permute-start | bytes 1775624 | tf_op jit(solution)/shard_map/ppermute | solution.py:61
  264.7 17.5 %collective-permute-start.52 = (bf16[10,16,1088]{2,1,0:T(8,128)(2,1)}, bf16[10,16,1088]{2,1,0:T(8,128)(2,1)}, u32[]{:S(2)}, u32[]{:S(2)}) collective-permute-start(bf16[10,16,1088]{2,1,0:T(8,128)(2,1)} %bitcast.119), channel_id=1, source_target_pairs={{8,0},{12,4},{16,8},{20,12},{24,16},{28,20},{0,24},{4,28},{9,1},{1... | collective-permute-start | bytes 1044488 | tf_op jit(solution)/shard_map/ppermute | solution.py:61
  268.4 22.4 %collective-permute-start.53 = (bf16[10,16,1088]{2,1,0:T(8,128)(2,1)}, bf16[10,16,1088]{2,1,0:T(8,128)(2,1)}, u32[]{:S(2)}, u32[]{:S(2)}) collective-permute-start(bf16[10,16,1088]{2,1,0:T(8,128)(2,1)} %bitcast.121), channel_id=1, source_target_pairs={{16,0},{20,4},{24,8},{28,12},{0,16},{4,20},{8,24},{12,28},{17,1},{... | collective-permute-start | bytes 1044488 | tf_op jit(solution)/shard_map/ppermute | solution.py:61
  268.8 22.0 %collective-permute-start.55 = (bf16[10,16,1088]{2,1,0:T(8,128)(2,1)}, bf16[10,16,1088]{2,1,0:T(8,128)(2,1)}, u32[]{:S(2)}, u32[]{:S(2)}) collective-permute-start(bf16[10,16,1088]{2,1,0:T(8,128)(2,1)} %bitcast.125), channel_id=1, source_target_pairs={{0,4},{4,0},{8,12},{12,8},{16,20},{20,16},{24,28},{28,24},{1,5},{5... | collective-permute-start | bytes 1044488 | tf_op jit(solution)/shard_map/ppermute | solution.py:61
  (106 other events, 1327.2 us)
